TPU v7x, 32 devices: a whole 2x2x4 slice. The times are simulated.
32 devices in a mesh: dp: 16 (over z, y, x), mp: 2 (over core).
Axes of the slice: x: 2, y: 2, z: 4, core: 2. Of those that a mesh axis runs over, the one named last changes fastest.
Arguments:
- tokens: bfloat16 [48, 2048, 768], P('dp', None, 'mp'), may hold values from -6 to 6
- segments: int32 [48, 2048], P('dp'), may hold values from 0 to 3, never falling along the last dimension, each value on 1 to 1024 neighbouring positions
- present: int32 [48, 2048], P('dp'), may hold values 0 or 1
- chosen: int32 [48, 256], P('dp'), may hold values from 0 to 2047, as said below
- attention: bfloat16 [3, 768, 768], P(None, 'dp', 'mp'), may hold values from -0.21875 to 0.21875
- mixing: bfloat16 [768, 768], P('mp', 'dp'), may hold values from -0.875 to 0.875
- expand: bfloat16 [768, 3072], P('dp', 'mp'), may hold values from -0.21875 to 0.21875
- contract: bfloat16 [3072, 768], P('mp', 'dp'), may hold values from -0.109375 to 0.109375
- prenorm: bfloat16 [768], P('dp'), may hold values from 0.5 to 1.5
- midnorm: bfloat16 [768], P('dp'), may hold values from 0.5 to 1.5
- router: bfloat16 [768], P('dp'), may hold values from -0.21875 to 0.21875
- cotangent: bfloat16 [48, 2048, 768], P('dp', None, 'mp'), may hold values from -6 to 6
Outputs:
- result: bfloat16 [48, 2048, 768], P('dp', None, 'mp')
- tokens_grad: bfloat16 [48, 2048, 768], P('dp', None, 'mp')
- attention_grad: float32 [3, 768, 768], P(None, 'dp', 'mp')
- mixing_grad: float32 [768, 768], P('mp', 'dp')
- expand_grad: float32 [768, 3072], P('dp', 'mp')
- contract_grad: float32 [3072, 768], P('mp', 'dp')
- prenorm_grad: float32 [768], P('dp')
- midnorm_grad: float32 [768], P('dp')
- router_grad: float32 [768], P('dp')
Inputs may be any that keep to these rules, and one draw needn't show every extreme that they name: `chosen`: in each row the 256 entries are distinct positions in increasing order.
All inputs are finite; a program needn't handle non-finite values. No bound on the sum of `present` on one device may be relied on, other than what follows from the above.
Results may differ from a plain program's by a relative error of at most 0.017.
Values may be sent and summed in bfloat16 or wider, within the bound.
No kernel may reach another device: no remote copies, remote signals or barrier semaphores. Data moves between devices by JAX's collectives and lax.ppermute only.
A program may use at most 192 MiB of HBM per device.

v0:
```python
import functools
import math

import jax
import jax.numpy as jnp
from jax import lax
from jax.experimental import pallas as pl
from jax.experimental.pallas import tpu as pltpu
from jax.sharding import PartitionSpec as P

HD = 64
EPSILON = 1e-06
BF = jnp.bfloat16
F32 = jnp.float32
VMEM_SPARE = 10 << 20


def mm(a, b):
    return jnp.dot(a, b, preferred_element_type=F32)


def mm_nt(a, b):
    return lax.dot_general(a, b, (((1,), (1,)), ((), ())), preferred_element_type=F32)


def mm_tn(a, b):
    return lax.dot_general(a, b, (((0,), (0,)), ((), ())), preferred_element_type=F32)


def inverse_rms(values):
    return lax.rsqrt(jnp.mean(values * values, axis=-1, keepdims=True) + EPSILON)


def call(kernel, outs, args, after=(), bits=None, scratch=(), flops=0, name=None):
    moved = sum(v.size * v.dtype.itemsize for v in (*args, *outs))
    scalars = [] if bits is None else [bits]
    count = len(scalars) + len(args)

    def body(*refs):
        kernel(*refs[:count], *refs[count + len(after) :])

    return pl.pallas_call(
        body,
        out_shape=outs,
        in_specs=[pl.BlockSpec(memory_space=pltpu.SMEM)] * len(scalars)
        + [pl.BlockSpec(memory_space=pltpu.VMEM)] * len(args)
        + [pl.BlockSpec(memory_space=pl.ANY)] * len(after),
        out_specs=[pl.BlockSpec(memory_space=pltpu.VMEM)] * len(outs),
        scratch_shapes=scratch,
        compiler_params=pltpu.CompilerParams(vmem_limit_bytes=VMEM_SPARE),
        cost_estimate=pl.CostEstimate(flops=flops, bytes_accessed=moved, transcendentals=0),
        name=name,
    )(*scalars, *args, *after)


def shape(dims, dtype=BF):
    return jax.ShapeDtypeStruct(tuple(dims), dtype)


def first_head(width=2 * HD):
    return lax.broadcasted_iota(jnp.int32, (1, width), 1) < HD


def attention_forward(rows, sel, states_ref, weights_ref, bias_ref, normed_ref, packed_ref, probs_ref, context_ref, gains_ref):
    width = states_ref.shape[1]
    half = context_ref.shape[1]
    gains_ref[...] = weights_ref[:, 4 * half :].astype(F32).T[:8]
    gain = gains_ref[0:1, :]
    scale = HD ** (-0.5)

    for row in range(rows):
        here = slice(row * sel, (row + 1) * sel)
        states = states_ref[here, :].astype(F32)
        normed_ref[here, :] = (states * inverse_rms(states) * gain).astype(BF)
    for start in range(0, 3 * half, 384):
        packed_ref[:, start : start + 384] = mm(normed_ref[...], weights_ref[:, start : start + 384]).astype(BF)
    first = first_head()

    @pl.loop(0, rows, unroll=True)
    def _(row):
        here = pl.ds(pl.multiple_of(row * sel, sel), sel)
        bias = bias_ref[row]
        for pair in range(half // (2 * HD)):
            at = pair * 2 * HD
            queries = packed_ref[here, at : at + 2 * HD]
            keys = packed_ref[here, half + at : half + at + 2 * HD]
            vals = packed_ref[here, 2 * half + at : 2 * half + at + 2 * HD]
            found = []
            for head in range(2):
                mine = first if head == 0 else ~first
                scores = mm_nt(jnp.where(mine, queries, jnp.zeros_like(queries)), keys) * scale + bias
                exponent = jnp.exp(scores - jnp.max(scores, axis=-1, keepdims=True))
                probs = exponent / jnp.sum(exponent, axis=-1, keepdims=True)
                probs_ref[row, 2 * pair + head] = probs
                found.append(mm(probs.astype(BF), vals))
            context_ref[here, at : at + 2 * HD] = jnp.where(first, found[0], found[1]).astype(BF)


def mix_forward(context_ref, mix_ref, out_ref):
    out_ref[...] = mm_nt(context_ref[...], mix_ref[...]).astype(BF)


def up_forward(
    rows, sel, states_ref, upstream_ref, own_ref, other_ref, up_ref, gains_ref, keep_ref,
    normed_ref, activated_ref, slope_ref, feed_grad_ref, grad_ref,
):
    mid_gain, router = gains_ref[1:2, :], gains_ref[2:3, :]
    c, a = (2.0 / math.pi) ** 0.5, 0.044715

    @pl.loop(0, rows)
    def _(row):
        here = pl.ds(pl.multiple_of(row * sel, sel), sel)
        states = states_ref[here, :].astype(F32)
        prob = jax.nn.sigmoid(jnp.sum(states * router, axis=-1, keepdims=True))
        gate = prob * keep_ref[here, :]
        feed_grad_ref[here, :] = (gate * upstream_ref[here, :].astype(F32)).astype(BF)
        middle = states + (own_ref[here, :].astype(F32) + other_ref[here, :].astype(F32))
        normed = (middle * inverse_rms(middle) * mid_gain).astype(BF)
        normed_ref[here, :] = normed

    upright_grad = feed_grad_ref[...].T
    chunk = 256
    for at in range(0, up_ref.shape[1], chunk):
        here = slice(at, at + chunk)
        hidden = mm(normed_ref[...], up_ref[:, here])
        square = hidden * hidden
        share = 0.5 * jnp.tanh(hidden * (c + c * a * square)) + 0.5
        activated = hidden * share
        activated_ref[:, here] = activated.astype(BF)
        slope = share + activated * (1.0 - share) * (2.0 * c + 6.0 * a * c * square)
        slope_ref[:, here] = slope.astype(BF)
        grad_ref[:, here] = mm(upright_grad, activated_ref[:, here]).astype(BF)


def down_backward(feed_grad_ref, down_ref, slope_ref, up_ref, hidden_grad_ref, out_ref):
    chunk = 256
    for at in range(0, down_ref.shape[1], chunk):
        here = slice(at, at + chunk)
        act_grad = mm(feed_grad_ref[...], down_ref[:, here])
        hidden_grad_ref[:, here] = (act_grad * slope_ref[:, here].astype(F32)).astype(BF)
    for at in range(0, out_ref.shape[1], chunk):
        here = slice(at, at + chunk)
        out_ref[:, here] = mm_nt(hidden_grad_ref[...], up_ref[here, :]).astype(BF)


def down_forward(normed_ref, hidden_grad_ref, activated_ref, down_ref, grad_ref, out_ref):
    upright_normed = normed_ref[...].T
    chunk = 256
    for at in range(0, grad_ref.shape[1], chunk):
        here = slice(at, at + chunk)
        grad_ref[:, here] = mm(upright_normed, hidden_grad_ref[:, here]).astype(BF)
    for at in range(0, out_ref.shape[1], chunk):
        here = slice(at, at + chunk)
        out_ref[:, here] = mm_nt(activated_ref[...], down_ref[here, :]).astype(BF)


def norm_backward(values, grads, gain):
    rho = inverse_rms(values)
    unit = values * rho
    scaled = grads * gain
    back = rho * (scaled - unit * jnp.mean(scaled * unit, axis=-1, keepdims=True))
    return back, jnp.sum(grads * unit, axis=0, keepdims=True)


def attention_backward(
    rows, sel, states_ref, own_ref, other_ref, mid_own_ref, mid_other_ref, upstream_ref, keep_ref, gains_ref,
    mix_ref, weights_ref, packed_ref, probs_ref,
    mixed_ref, packed_grad_ref, out_ref, middle_grad_ref, gain_grad_ref, context_grad_ref,
):
    mid_gain, router = gains_ref[1:2, :], gains_ref[2:3, :]
    half = mix_ref.shape[1]
    scale = HD ** (-0.5)
    gain_grad_ref[...] = jnp.zeros_like(gain_grad_ref)

    @pl.loop(0, rows)
    def _(row):
        here = pl.ds(pl.multiple_of(row * sel, sel), sel)
        states = states_ref[here, :].astype(F32)
        middle = states + (own_ref[here, :].astype(F32) + other_ref[here, :].astype(F32))
        mid_in = mid_own_ref[here, :].astype(F32) + mid_other_ref[here, :].astype(F32)
        middle_grad, gain_grad = norm_backward(middle, mid_in, mid_gain)
        gain_grad_ref[0:1, :] += gain_grad
        middle_grad_ref[here, :] = middle_grad
        gate = jax.nn.sigmoid(jnp.sum(states * router, axis=-1, keepdims=True)) * keep_ref[here, :]
        mixed = (gate * upstream_ref[here, :].astype(F32) + middle_grad).astype(BF)
        mixed_ref[here, :] = mixed

    context_grad_ref[...] = mm(mixed_ref[...], mix_ref[...]).astype(BF)
    first = first_head()

    @pl.loop(0, rows, unroll=True)
    def _(row):
        here = pl.ds(pl.multiple_of(row * sel, sel), sel)
        for pair in range(half // (2 * HD)):
            at = pair * 2 * HD
            queries = packed_ref[here, at : at + 2 * HD]
            keys = packed_ref[here, half + at : half + at + 2 * HD]
            vals = packed_ref[here, 2 * half + at : 2 * half + at + 2 * HD]
            grads = context_grad_ref[here, at : at + 2 * HD]
            queries_up, grads_up = queries.T, grads.T
            by_query, by_key, by_value = [], [], []
            for head in range(2):
                mine = first if head == 0 else ~first
                lanes = slice(head * HD, (head + 1) * HD)
                probs = probs_ref[row, 2 * pair + head]
                prob_grad = mm_nt(jnp.where(mine, grads, jnp.zeros_like(grads)), vals)
                centre = jnp.sum(probs * prob_grad, axis=-1, keepdims=True)
                score_grad = (probs * (prob_grad - centre)).astype(BF)
                by_query.append(mm(score_grad, keys))
                by_key.append(mm(queries_up[lanes], score_grad))
                by_value.append(mm(grads_up[lanes], probs.astype(BF)))
            packed_grad_ref[here, at : at + 2 * HD] = (
                jnp.where(first, by_query[0], by_query[1]) * scale
            ).astype(BF)
            packed_grad_ref[here, half + at : half + at + 2 * HD] = (
                (jnp.concatenate(by_key, axis=0) * scale).astype(BF).T
            )
            packed_grad_ref[here, 2 * half + at : 2 * half + at + 2 * HD] = (
                jnp.concatenate(by_value, axis=0).astype(BF).T
            )

    chunk = 256
    for at in range(0, out_ref.shape[1], chunk):
        here = slice(at, at + chunk)
        out_ref[:, here] = mm_nt(packed_grad_ref[...], weights_ref[here, : 3 * half]).astype(BF)


def projection_grads(normed_ref, packed_grad_ref, mixed_ref, context_ref, grad_ref):
    wide, chunk = packed_grad_ref.shape[1], 384
    upright_normed, upright_mixed = normed_ref[...].T, mixed_ref[...].T
    for at in range(0, wide, chunk):
        here = slice(at, at + chunk)
        grad_ref[:, here] = mm(upright_normed, packed_grad_ref[:, here]).astype(BF)
    grad_ref[:, wide:] = mm(upright_mixed, context_ref[...]).astype(BF)


def final_forward(
    rows, sel, states_ref, upstream_ref, own_ref, other_ref, feed_own_ref, feed_other_ref, gains_ref, keep_ref,
    finished_ref, logit_grad_ref, router_grad_ref,
):
    router = gains_ref[2:3, :]
    router_grad_ref[...] = jnp.zeros_like(router_grad_ref)

    @pl.loop(0, rows)
    def _(row):
        here = pl.ds(pl.multiple_of(row * sel, sel), sel)
        states = states_ref[here, :].astype(F32)
        attended = own_ref[here, :].astype(F32) + other_ref[here, :].astype(F32)
        branch = attended + (feed_own_ref[here, :].astype(F32) + feed_other_ref[here, :].astype(F32))
        prob = jax.nn.sigmoid(jnp.sum(states * router, axis=-1, keepdims=True))
        keep = keep_ref[here, :]
        finished_ref[here, :] = (states + prob * keep * branch).astype(BF)
        gate_grad = jnp.sum(upstream_ref[here, :].astype(F32) * branch, axis=-1, keepdims=True)
        logit_grad = gate_grad * keep * prob * (1.0 - prob)
        logit_grad_ref[here, :] = logit_grad
        router_grad_ref[0:1, :] += jnp.sum(logit_grad * states, axis=0, keepdims=True)


def final_backward(
    rows, sel, states_ref, upstream_ref, middle_grad_ref, pre_own_ref, pre_other_ref, logit_grad_ref, gains_ref,
    mid_gain_grad_ref, router_grad_ref, total_ref, vectors_ref, lines_ref,
):
    pre_gain, router = gains_ref[0:1, :], gains_ref[2:3, :]
    lines_ref[...] = jnp.zeros_like(lines_ref)
    lines_ref[1:2, :] = mid_gain_grad_ref[0:1, :]
    lines_ref[2:3, :] = router_grad_ref[0:1, :]

    @pl.loop(0, rows)
    def _(row):
        here = pl.ds(pl.multiple_of(row * sel, sel), sel)
        states = states_ref[here, :].astype(F32)
        pre_in = pre_own_ref[here, :].astype(F32) + pre_other_ref[here, :].astype(F32)
        back, gain_grad = norm_backward(states, pre_in, pre_gain)
        lines_ref[0:1, :] += gain_grad
        total = upstream_ref[here, :].astype(F32) + logit_grad_ref[here, :] * router
        total_ref[here, :] = (total + middle_grad_ref[here, :] + back).astype(BF)

    vectors_ref[...] = lines_ref[...].T.astype(BF)


def upright(row):
    return jnp.broadcast_to(row, (8, row.shape[1])).T[:, :1]


def one_hot_rows(chosen_ref, sel, length):
    row = pl.ds(pl.program_id(0), 1)
    chosen = upright(chosen_ref[row, :].astype(F32)).astype(jnp.int32)
    return jnp.where(chosen == lax.broadcasted_iota(jnp.int32, (sel, length), 1), 1.0, 0.0).astype(BF)


def pick_rows(base_ref, chosen_ref, picked_ref):
    one_hot = one_hot_rows(chosen_ref, picked_ref.shape[1], base_ref.shape[1])
    picked_ref[0] = mm(one_hot, base_ref[0]).astype(BF)


def pick_and_mask(base_ref, chosen_ref, segments_ref, present_ref, picked_ref, bias_ref, keep_ref):
    sel, length = picked_ref.shape[1], base_ref.shape[1]
    row = pl.ds(pl.program_id(0), 1)
    one_hot = one_hot_rows(chosen_ref, sel, length)
    picked_ref[0] = mm(one_hot, base_ref[0]).astype(BF)
    both = jnp.concatenate(
        [segments_ref[row, :].astype(F32), present_ref[row, :].astype(F32), jnp.zeros((6, length), F32)], axis=0
    ).astype(BF)
    along = mm_nt(both, one_hot)
    down = along.T
    slot = lax.broadcasted_iota(jnp.int32, (sel, sel), 0)
    seen = lax.broadcasted_iota(jnp.int32, (sel, sel), 1)
    open_key = (along[1:2, :] > 0.5) | (slot == seen)
    permitted = (seen <= slot) & (down[:, 0:1] == along[0:1, :]) & open_key
    bias_ref[0] = jnp.where(permitted, 0.0, -1e30)
    keep_ref[...] = down[:, 1:2]


def select(base, tables, mask=False, after=()):
    rows, length, half = base.shape
    sel = tables[0].shape[1]
    count = 1 + len(tables)
    kernel = pick_and_mask if mask else pick_rows

    def body(*refs):
        kernel(*refs[:count], *refs[count + len(after) :])

    outs = [shape((rows, sel, half)), shape((rows, sel, sel), F32), shape((rows * sel, 1), F32)]
    specs = [
        pl.BlockSpec((1, sel, half), lambda row: (row, 0, 0)),
        pl.BlockSpec((1, sel, sel), lambda row: (row, 0, 0)),
        pl.BlockSpec((sel, 1), lambda row: (row, 0)),
    ]
    return pl.pallas_call(
        body,
        grid=(rows,),
        out_shape=outs if mask else outs[:1],
        in_specs=[pl.BlockSpec((1, length, half), lambda row: (row, 0, 0))]
        + [pl.BlockSpec(v.shape, lambda row: (0, 0)) for v in tables]
        + [pl.BlockSpec(memory_space=pl.ANY)] * len(after),
        out_specs=specs if mask else specs[:1],
        compiler_params=pltpu.CompilerParams(vmem_limit_bytes=2 * VMEM_SPARE),
        cost_estimate=pl.CostEstimate(
            flops=2 * rows * sel * length * half, bytes_accessed=2 * base.size, transcendentals=0
        ),
        name="select_rows",
    )(base, *tables, *after)


def put_rows(bits_ref, chosen_ref, values_ref, base_ref, out_ref):
    long, half = out_ref.shape[1:]
    sel = values_ref.shape[0]
    first = pl.program_id(1) * long
    chosen = chosen_ref[pl.ds(pl.program_id(0), 1), :]
    hit = first + lax.broadcasted_iota(jnp.int32, (long, sel), 0) == chosen
    one_hot = jnp.where(hit, 1.0, 0.0).astype(BF)
    offset = pl.multiple_of(bits_ref[-1 + bits_ref.shape[0]] * half, half)
    values = values_ref[:, pl.ds(offset, half)]
    placed = mm(one_hot, jnp.concatenate([values, jnp.ones((sel, 128), BF)], axis=1))
    taken = placed[:, half:] > 0.5
    for at in range(0, half, 128):
        here = slice(at, at + 128)
        out_ref[0, :, here] = jnp.where(taken, placed[:, here].astype(BF), base_ref[0, :, here])


def put(base, chosen, values, bits, after=()):
    rows, length, half = base.shape
    sel = chosen.shape[1]
    long = length // 2

    def body(*refs):
        put_rows(*refs[:4], refs[-2])
        refs[-1][...] = jnp.zeros_like(refs[-1])

    return pl.pallas_call(
        body,
        grid=(rows, length // long),
        out_shape=(shape(base.shape), shape((8, 128), F32)),
        in_specs=[
            pl.BlockSpec(memory_space=pltpu.SMEM),
            pl.BlockSpec(chosen.shape, lambda row, part: (0, 0)),
            pl.BlockSpec((sel, values.shape[1]), lambda row, part: (row, 0)),
            pl.BlockSpec((1, long, half), lambda row, part: (row, part, 0)),
        ]
        + [pl.BlockSpec(memory_space=pl.ANY)] * len(after),
        out_specs=[
            pl.BlockSpec((1, long, half), lambda row, part: (row, part, 0)),
            pl.BlockSpec((8, 128), lambda row, part: (0, 0)),
        ],
        compiler_params=pltpu.CompilerParams(vmem_limit_bytes=24 << 20),
        cost_estimate=pl.CostEstimate(
            flops=2 * rows * sel * length * half, bytes_accessed=4 * base.size, transcendentals=0
        ),
        name="put_rows",
    )(bits, chosen, values, base, *after)


def first_columns(attention_ref, mixing_ref, vectors_ref, out_ref):
    half = attention_ref.shape[2]
    for k in range(3):
        out_ref[:, k * half : (k + 1) * half] = attention_ref[k]
    out_ref[:, 3 * half : 4 * half] = mixing_ref[...]
    out_ref[:, 4 * half :] = vectors_ref[...]


def second_columns(cuts, expand_ref, contract_ref, out_ref):
    at = 0
    for start, end in cuts:
        out_ref[:, at : at + end - start] = expand_ref[:, start:end]
        at += end - start
        out_ref[:, at : at + end - start] = contract_ref[:, start:end]
        at += end - start


def untouched(*refs):
    pass


def tie(value, *others):
    if not others:
        return value
    anywhere = pl.BlockSpec(memory_space=pl.ANY)
    return pl.pallas_call(
        untouched,
        out_shape=jax.ShapeDtypeStruct(value.shape, value.dtype),
        in_specs=[anywhere] * (1 + len(others)),
        out_specs=anywhere,
        input_output_aliases={0: 0},
        compiler_params=pltpu.CompilerParams(vmem_limit_bytes=1 << 20),
        cost_estimate=pl.CostEstimate(flops=0, bytes_accessed=0, transcendentals=0),
    )(value, *others)


class Cube:
    def __init__(self, count):
        self.count, self.depth = count, count.bit_length() - 1
        index = lax.axis_index("dp").astype(jnp.int32)
        self.bits = jnp.append(
            (index >> jnp.arange(self.depth)) & 1, lax.axis_index("mp").astype(jnp.int32)
        )
        short = self.depth // 3
        self.x, self.y = list(range(short)), list(range(short, 2 * short))
        self.z = list(range(2 * short, self.depth))
        self.far = self.z[1:]
        near = [self.x, self.y, self.z[:1]]
        self.orders = [sum(near[k:] + near[:k], []) for k in range(3)]

    def swap(self, value, bit):
        return lax.ppermute(value, "dp", [(i, i ^ (1 << bit)) for i in range(self.count)])


class Part:
    def __init__(self, value, bits, sent=None, start=0, width=None):
        self.value, self.bits, self.sent = value, list(bits), sent
        self.start, self.width = start, width or value.shape[2]

    def columns(self, start, end):
        return Part(self.value, self.bits, self.sent, self.start + start, end - start)


def thirds(width):
    ends = [(k * width // 3 + 64) // 128 * 128 for k in range(4)]
    return list(zip(ends, ends[1:]))


def start_exchange(cube, part, bit):
    part.sent = cube.swap(part.value, bit)
    return part


def stack_parts(plan, bits_ref, *refs):
    ins, outs = refs[: 2 * len(plan)], refs[2 * len(plan) :]
    for k, (bit, blocks) in enumerate(plan):
        mine = bits_ref[bit]
        for block in range(blocks):
            outs[k][mine, block] = ins[2 * k][block]
            outs[k][1 - mine, block] = ins[2 * k + 1][block]


def stack(cube, parts, bits, after=()):
    outs, args, plan = [], [], []
    for part, bit in zip(parts, bits):
        outs.append(shape((2,) + part.value.shape))
        args += [part.value, part.sent]
        plan.append((bit, part.value.shape[0]))
    found = call(functools.partial(stack_parts, plan), outs, args, after, cube.bits, name="stack_parts")
    return [
        Part(v.reshape((-1,) + v.shape[2:]), [bit] + part.bits) for v, part, bit in zip(found, parts, bits)
    ]


def split_columns(plan, own_ref, *out_refs):
    for ref, (start, end) in zip(out_refs, plan):
        ref[...] = own_ref[:, :, start:end]


def whole_rows(plan, bits_ref, *refs):
    ins, out_ref = refs[:-1], refs[-1]
    column = 0
    for k, (bit, places, start, width) in enumerate(plan):
        mine = bits_ref[bit]
        for block, place in enumerate(places):
            here = slice(column, column + width)
            out_ref[place + (mine << bit), :, here] = ins[2 * k][block, :, start : start + width]
            out_ref[place + ((1 - mine) << bit), :, here] = ins[2 * k + 1][block, :, start : start + width]
        column += width


def whole(cube, parts, bits, after=()):
    args, plan, width = [], [], 0
    for part, bit in zip(parts, bits):
        places = []
        for block in range(part.value.shape[0]):
            digits = [(block >> k) & 1 for k in range(len(part.bits))][::-1]
            places.append(sum(digit << b for digit, b in zip(digits, part.bits)))
        args += [part.value, part.sent]
        plan.append((bit, places, part.start, part.width))
        width += part.width
    rows = parts[0].value.shape[1]
    (found,) = call(
        functools.partial(whole_rows, plan),
        (shape((cube.count, rows, width)),),
        args,
        after,
        cube.bits,
        name="whole_rows",
    )
    return found.reshape(-1, width)


def fold_parts(plan, bits_ref, *refs):
    refs = list(refs)
    taken = [[(refs.pop(0), refs.pop(0) if sent else None) for sent, _, _ in sources] for _, _, sources in plan]
    for (bit, (high, low), sources), ins in zip(plan, taken):
        sent_ref, kept_ref = refs.pop(0), refs.pop(0)
        mine = bits_ref[bit]
        column = 0
        for (_, start, width), (value_ref, other_ref) in zip(sources, ins):
            there = slice(start, start + width)
            here = slice(column, column + width)
            for a in range(high):
                for b in range(low):
                    for index, out_ref in ((1 - mine, sent_ref), (mine, kept_ref)):
                        found = value_ref[a, index, b, :, there].astype(F32)
                        if other_ref is not None:
                            found += other_ref[a, index, b, :, there].astype(F32)
                        out_ref[a * low + b, :, here] = found.astype(out_ref.dtype)
            column += width


def fold(cube, groups, bits, after=()):
    args, outs, plan = [], [], []
    for sources, bit in zip(groups, bits):
        at = sources[0].bits.index(bit)
        high, low = 1 << at, 1 << (len(sources[0].bits) - at - 1)
        listed = []
        for part in sources:
            for value in (part.value, part.sent):
                if value is not None:
                    args.append(value.reshape((high, 2, low) + value.shape[1:]))
            listed.append((part.sent is not None, part.start, part.width))
        plan.append((bit, (high, low), listed))
        dims = (high * low, sources[0].value.shape[1], sum(p.width for p in sources))
        outs += [shape(dims), shape(dims, F32)]
    found = call(functools.partial(fold_parts, plan), outs, args, after, cube.bits, name="fold_parts")
    done = []
    for k, (sources, bit) in enumerate(zip(groups, bits)):
        left = [b for b in sources[0].bits if b != bit]
        done.append(Part(found[2 * k + 1], left, cube.swap(found[2 * k], bit)))
    return done


def cut(cube, total):
    blocks = total.reshape(cube.count, -1, total.shape[1])
    bits = list(range(cube.depth))[::-1]
    return [Part(blocks, bits, None, start, end - start) for start, end in thirds(total.shape[1]) if end > start]


def arrived(parts):
    return [p.sent for p in parts]


def sum_first(value_ref, sent_ref, attention_ref, mixing_ref, vectors_ref):
    half = attention_ref.shape[2]
    total = value_ref[0] + sent_ref[0].astype(F32)
    for k in range(3):
        attention_ref[k] = total[:, k * half : (k + 1) * half]
    mixing_ref[...] = total[:, 3 * half : 4 * half]
    vectors_ref[...] = total[:, 4 * half :].T


def sum_second(cuts, value_ref, sent_ref, expand_ref, contract_ref):
    at = 0
    for start, end in cuts:
        for side in range(2):
            width = end - start
            total = value_ref[0, :, at : at + width] + sent_ref[0, :, at : at + width].astype(F32)
            (expand_ref if side else contract_ref)[:, start:end] = total
            at += width


def other_core(value):
    return lax.ppermute(value, "mp", [(0, 1), (1, 0)])


def both_halves(value):
    other = other_core(value)
    low = lax.axis_index("mp") == 0
    return jnp.concatenate([jnp.where(low, value, other), jnp.where(low, other, value)], axis=-1)


def shards(
    tokens,
    segments,
    present,
    chosen,
    attention,
    mixing,
    expand,
    contract,
    prenorm,
    midnorm,
    router,
    cotangent,
    count,
):
    cube = Cube(count)
    row_count, length, half_width = tokens.shape
    sel_count = chosen.shape[1]
    token_count = row_count * sel_count
    own_rows = mixing.shape[1]
    width = 2 * half_width
    hidden_here = expand.shape[1]
    heads_here = half_width // HD
    by_row = (row_count, sel_count)

    vectors = jnp.pad(jnp.stack([prenorm, midnorm, router], axis=1), ((0, 0), (0, 125)))
    cuts = thirds(hidden_here)
    (first_own,) = call(
        first_columns, (shape((own_rows, 4 * half_width + 128)),), (attention, mixing.T, vectors), name="first_columns"
    )
    first_far = start_exchange(cube, Part(first_own[None], []), cube.far[-1])
    (second_own,) = call(
        functools.partial(second_columns, cuts),
        (shape((own_rows, 2 * hidden_here)),),
        (expand, contract.T),
        name="second_columns",
    )
    picked, bias, keep = select(tokens, [chosen, segments, present], True)

    def spread(far, after, begin=()):
        for bit in cube.far[-2::-1]:
            far = start_exchange(cube, stack(cube, [far], [far_bit(far)], after)[0], bit)
        column = stack(cube, [far], [far_bit(far)], after)[0]
        ends = thirds(column.width)
        found = call(
            functools.partial(split_columns, ends),
            [shape(column.value.shape[:2] + (end - start,)) for start, end in ends],
            [column.value],
            begin,
            name="split_columns",
        )
        return [Part(v, column.bits) for v in found]

    def far_bit(part):
        return cube.far[-1 - len(part.bits)]

    def step_bits(step):
        return [order[step] for order in cube.orders]

    def send(parts, step):
        return [start_exchange(cube, p, bit) for p, bit in zip(parts, step_bits(step))]

    steps = len(cube.orders[0])
    first_parts = spread(first_far, [picked])
    states = both_halves(tie(picked, first_parts[0].value)).reshape(token_count, width)
    first_parts = send(first_parts, 0)
    second_far = start_exchange(cube, Part(tie(second_own, *arrived([first_far]))[None], []), cube.far[-1])
    for step in range(1, steps):
        if step == steps - 1:
            (picked_grads,) = select(cotangent, [chosen], False, [first_parts[0].value])
            after = arrived([second_far]) + [picked_grads]
        else:
            after = [states] if step == 1 else []
        first_parts = send(stack(cube, first_parts, step_bits(step - 1), after), step)
    first_last = [p.value for p in first_parts]
    first = whole(cube, first_parts, step_bits(steps - 1))
    mix = first[:, 3 * half_width : 4 * half_width]
    second_parts = send(spread(second_far, [], first_last[:1]), 0)
    second_begun = []
    for step in range(1, steps - 1):
        second_parts = stack(cube, second_parts, step_bits(step - 1), [first] if step == 1 else [])
        second_begun = second_begun or [p.value for p in second_parts]
        second_parts = send(second_parts, step)
    upstream = both_halves(tie(picked_grads, *second_begun)).reshape(token_count, width)
    second_parts = stack(cube, second_parts, step_bits(steps - 2))
    each = hidden_here // 3
    up_parts, down_parts = [], []
    for p in second_parts:
        up_parts.append(Part(p.value[..., :each], p.bits))
        down_parts.append(Part(p.value[..., each:], p.bits))
    up = whole(cube, send(up_parts, steps - 1), step_bits(steps - 1))
    down_parts = send(down_parts, steps - 1)

    wide = shape((token_count, width))
    tall = shape((token_count, hidden_here))
    vector = shape((8, width), F32)
    normed, packed, probs, context, gains = call(
        functools.partial(attention_forward, *by_row),
        (
            wide,
            shape((token_count, 3 * half_width)),
            shape((row_count, heads_here, sel_count, sel_count), F32),
            shape((token_count, half_width)),
            vector,
        ),
        (states, first, bias),
        after=second_begun,
        flops=token_count * width * half_width * 6,
        name="attention_forward",
    )
    (att_own,) = call(
        mix_forward, (wide,), (context, mix), flops=2 * token_count * width * half_width, name="mix_forward"
    )
    att_other = other_core(att_own)
    normed_mid, activated, slope, feed_grad, down_grad = call(
        functools.partial(up_forward, *by_row),
        (wide, tall, tall, wide, shape((width, hidden_here))),
        (states, upstream, att_own, att_other, up, gains, keep),
        flops=4 * token_count * width * hidden_here,
        name="up_forward",
    )
    down = whole(cube, down_parts, step_bits(steps - 1), [activated])

    hidden_grad, mid_own = call(
        down_backward,
        (tall, wide),
        (feed_grad, down, slope, up),
        flops=4 * token_count * width * hidden_here,
        name="down_backward",
    )
    up_grad, feed_own = call(
        down_forward,
        (shape((width, hidden_here)), wide),
        (normed_mid, hidden_grad, activated, down),
        flops=4 * token_count * width * hidden_here,
        name="down_forward",
    )
    feed_other = other_core(feed_own)
    mid_other = tie(other_core(mid_own), feed_own)

    def back_bits(step):
        return [order[-1 - step] for order in cube.orders]

    def alone(parts):
        return [[p] for p in parts]

    both_grads = [list(pair) for pair in zip(cut(cube, down_grad), cut(cube, up_grad))]
    both_grads = fold(cube, both_grads, back_bits(0))

    mixed, packed_grad, pre_own, middle_grad, mid_gain_grad = call(
        functools.partial(attention_backward, *by_row),
        (
            wide,
            shape((token_count, 3 * half_width)),
            wide,
            shape((token_count, width), F32),
            vector,
        ),
        (states, att_own, att_other, mid_own, mid_other, upstream, keep, gains, mix, first, packed, probs),
        after=[both_grads[0].value],
        scratch=[pltpu.VMEM((token_count, half_width), BF)],
        flops=10 * token_count * width * half_width,
        name="attention_backward",
    )
    (first_grad,) = call(
        projection_grads,
        (shape((width, 4 * half_width)),),
        (normed, packed_grad, mixed, context),
        flops=8 * token_count * width * half_width,
        name="projection_grads",
    )
    both_grads = fold(cube, alone(both_grads), back_bits(1), [first_grad])
    pre_other = other_core(tie(pre_own, both_grads[0].value))
    finished, logit_grad, router_grad = call(
        functools.partial(final_forward, *by_row),
        (wide, shape((token_count, 1), F32), vector),
        (states, upstream, att_own, att_other, feed_own, feed_other, gains, keep),
        after=[both_grads[0].value],
        name="final_forward",
    )
    total_grad, vector_grads = call(
        functools.partial(final_backward, *by_row),
        (wide, shape((width, 128))),
        (states, upstream, middle_grad, pre_own, pre_other, logit_grad, gains, mid_gain_grad, router_grad),
        scratch=[pltpu.VMEM((128, width), F32)],
        name="final_backward",
    )
    first_grads = alone(cut(cube, first_grad))
    first_grads[-1] += cut(cube, vector_grads)
    first_grads = fold(cube, first_grads, back_bits(0))
    result, done = put(tokens, chosen, finished, cube.bits, [first_grads[0].value])
    tokens_grad, _ = put(cotangent, chosen, total_grad, cube.bits, [done])
    for step in range(2, steps):
        both_grads = fold(cube, alone(both_grads), back_bits(step), [first_grad] if step == 2 else [])
    for step in range(1, steps):
        first_grads = fold(cube, alone(first_grads), back_bits(step), [done] if step == 1 else [])
    both_grads, first_grads = [both_grads], [first_grads]
    for bit in cube.far:
        both_grads = [fold(cube, both_grads, [bit])]
        first_grads = [fold(cube, first_grads, [bit])]
    (both_grad,), (first_grad,) = both_grads[0], first_grads[0]
    up_out, down_out = call(
        functools.partial(sum_second, cuts),
        (shape((own_rows, hidden_here), F32),) * 2,
        (both_grad.value, both_grad.sent),
        name="sum_second",
    )
    attention_out, mixing_out, vector_out = call(
        sum_first,
        (
            shape((3, own_rows, half_width), F32),
            shape((own_rows, half_width), F32),
            shape((128, own_rows), F32),
        ),
        (first_grad.value, first_grad.sent),
        name="sum_first",
    )
    return (
        result,
        tokens_grad,
        attention_out,
        mixing_out.T,
        up_out,
        down_out.T,
        vector_out[0],
        vector_out[1],
        vector_out[2],
    )


def solution(mesh):
    in_specs = (
        P("dp", None, "mp"),
        P("dp", None),
        P("dp", None),
        P("dp", None),
        P(None, "dp", "mp"),
        P("mp", "dp"),
        P("dp", "mp"),
        P("mp", "dp"),
        P("dp"),
        P("dp"),
        P("dp"),
        P("dp", None, "mp"),
    )
    out_specs = (
        P("dp", None, "mp"),
        P("dp", None, "mp"),
        P(None, "dp", "mp"),
        P("mp", "dp"),
        P("dp", "mp"),
        P("mp", "dp"),
        P("dp"),
        P("dp"),
        P("dp"),
    )
    count = mesh.shape["dp"]

    def body(*args):
        return shards(*args, count)

    return jax.shard_map(body, mesh=mesh, in_specs=in_specs, out_specs=out_specs, check_vma=False)
```

profile of v0, /device:TPU:0, one launch (start us, length us, event | category | flops | bytes accessed | tf_op | source)
XLA Modules:
  0.0 176.3 jit_solution(871266720694166948)
XLA Ops:
  3.1 4.1 %collective-permute-start = (bf16[1,48,1664]{2,1,0:T(8,128)(2,1)S(1)}, bf16[1,48,1664]{2,1,0:T(8,128)(2,1)S(1)}, u32[]{:S(2)}, u32[]{:S(2)}) collective-permute-start(bf16[1,48,1664]{2,1,0:T(8,128)(2,1)S(1)} %bitcast.149), channel_id=1, source_target_pairs={{0,16},{2,18},{4,20},{6,22},{8,24},{10,26},{12,28},{14,30},{16,0},... | collective-permute-start | bytes 479240 | tf_op jit(solution)/shard_map/ppermute | solution.py:444
  7.3 2.3 %copy-done = bf16[3,2048,384]{2,1,0:T(8,128)(2,1)S(1)} copy-done((bf16[3,2048,384]{2,1,0:T(8,128)(2,1)S(1)}, bf16[3,2048,384]{2,1,0:T(8,128)(2,1)}, u32[]{:S(2)}) %copy-start) | copy-done | bytes 4718616
  11.9 3.9 %select_rows.2 = (bf16[3,256,384]{2,1,0:T(8,128)(2,1)S(1)}, f32[3,256,256]{2,1,0:T(8,128)S(1)}, f32[768,1]{1,0:T(8,128)S(1)}) custom-call(bf16[3,2048,384]{2,1,0:T(8,128)(2,1)S(1)} %copy-done, s32[3,256]{1,0:T(4,128)S(1)} %copy-done.4, s32[3,2048]{1,0:T(4,128)S(1)} %copy-done.7, s32[3,2048]{1,0:T(4,128)S(1)} %copy-done.8), custom_call_target="tpu_custom_call" | custom-call | flops 1207959552 | bytes 4718592 | tf_op jit(solution)/shard_map/select_rows/pallas_call | solution.py:329
  19.9 1.6 collective-permute-start.4
  25.3 2.5 %collective-permute-start.7 = (bf16[4,48,640]{2,1,0:T(8,128)(2,1)S(1)}, bf16[4,48,640]{2,1,0:T(8,128)(2,1)S(1)}, u32[]{:S(2)}, u32[]{:S(2)}) collective-permute-start(bf16[4,48,640]{2,1,0:T(8,128)(2,1)S(1)} %bitcast.168), channel_id=1, source_target_pairs={{0,8},{2,10},{4,12},{6,14},{8,0},{10,2},{12,4},{14,6},{16,24},{18,... | collective-permute-start | bytes 737288 | tf_op jit(solution)/shard_map/ppermute | solution.py:444
  28.9 2.9 %select_rows.3.refs_8_.refs_0_ = bf16[3,256,384]{2,1,0:T(8,128)(2,1)S(1)} custom-call(bf16[3,2048,384]{2,1,0:T(8,128)(2,1)S(1)} %bitcast.107, s32[3,256]{1,0:T(4,128)S(1)} %copy-done.5, bf16[4,48,512]{2,1,0:T(8,128)(2,1)S(1)} %bitcast.138), custom_call_target="tpu_custom_call" | custom-call | flops 1207959552 | bytes 4718592 | tf_op jit(solution)/shard_map/select_rows/pallas_call | solution.py:329
  31.7 5.3 %collective-permute-done.5.refs_2_.refs_7_ = bf16[1,48,3072]{2,1,0:T(8,128)(2,1)S(1)} collective-permute-done((bf16[1,48,3072]{2,1,0:T(8,128)(2,1)S(1)}, bf16[1,48,3072]{2,1,0:T(8,128)(2,1)S(1)}, u32[]{:S(2)}, u32[]{:S(2)}) %collective-permute-start.5) | collective-permute-done | bytes 294944 | tf_op jit(solution)/shard_map/ppermute | solution.py:444
  41.6 1.9 %collective-permute-start.11 = (bf16[2,48,1024]{2,1,0:T(8,128)(2,1)S(1)}, bf16[2,48,1024]{2,1,0:T(8,128)(2,1)S(1)}, u32[]{:S(2)}, u32[]{:S(2)}) collective-permute-start(bf16[2,48,1024]{2,1,0:T(8,128)(2,1)S(1)} %get-tuple-element.112.refs_5_), channel_id=1, source_target_pairs={{0,8},{2,10},{4,12},{6,14},{8,0},{10,2},{12,4},{14,6},{16,24},{18,... | collective-permute-start | bytes 589832 | tf_op jit(solution)/shard_map/ppermute | solution.py:444
  43.5 6.6 %collective-permute-done.12.refs_2_ = bf16[8,48,512]{2,1,0:T(8,128)(2,1)S(1)} collective-permute-done((bf16[8,48,512]{2,1,0:T(8,128)(2,1)S(1)}, bf16[8,48,512]{2,1,0:T(8,128)(2,1)S(1)}, u32[]{:S(2)}, u32[]{:S(2)}) %collective-permute-start.12) | collective-permute-done | bytes 393248 | tf_op jit(solution)/shard_map/ppermute | solution.py:444
  52.6 3.2 %collective-permute-done.9.refs_2_ = bf16[2,48,1024]{2,1,0:T(8,128)(2,1)S(1)} collective-permute-done((bf16[2,48,1024]{2,1,0:T(8,128)(2,1)S(1)}, bf16[2,48,1024]{2,1,0:T(8,128)(2,1)S(1)}, u32[]{:S(2)}, u32[]{:S(2)}) %collective-permute-start.9) | collective-permute-done | bytes 196640 | tf_op jit(solution)/shard_map/ppermute | solution.py:444
  57.9 4.8 %attention_forward.1 = (bf16[768,768]{1,0:T(8,128)(2,1)S(1)}, bf16[768,1152]{1,0:T(8,128)(2,1)S(1)}, f32[3,6,256,256]{3,2,1,0:T(8,128)S(1)}, bf16[768,384]{1,0:T(8,128)(2,1)S(1)}, f32[8,768]{1,0:T(8,128)S(1)}) custom-call(bf16[768,768]{1,0:T(8,128)(2,1)S(1)} %bitcast.89, bf16[768,1664]{1,0:T(8,128)(2,1)S(1)} %bitcast.86, ...), custom_call_target="tpu_custom_call" | custom-call | flops 1358954496 | bytes 12804096 | tf_op jit(solution)/shard_map/attention_forward/pallas_call | solution.py:42
  65.9 1.7 collective-permute-start.20
  70.6 7.4 %collective-permute-done.20.refs_2_ = bf16[8,48,512]{2,1,0:T(8,128)(2,1)S(1)} collective-permute-done((bf16[8,48,512]{2,1,0:T(8,128)(2,1)S(1)}, bf16[8,48,512]{2,1,0:T(8,128)(2,1)S(1)}, u32[]{:S(2)}, u32[]{:S(2)}) %collective-permute-start.20) | collective-permute-done | bytes 393248 | tf_op jit(solution)/shard_map/ppermute | solution.py:444
  78.5 1.7 collective-permute-start.25
  81.0 6.7 %up_forward.1 = (bf16[768,768]{1,0:T(8,128)(2,1)S(1)}, bf16[768,1536]{1,0:T(8,128)(2,1)S(1)}, bf16[768,1536]{1,0:T(8,128)(2,1)S(1)}, bf16[768,768]{1,0:T(8,128)(2,1)S(1)}, bf16[768,1536]{1,0:T(8,128)(2,1)S(1)}) custom-call(bf16[768,768]{1,0:T(8,128)(2,1)S(1)} %bitcast.90, bf16[768,768]{1,0:T(8,128)(2,1)S(1)} %bitcast.100, ...), custom_call_target="tpu_custom_call" | custom-call | flops 3623878656 | bytes 16542720 | tf_op jit(solution)/shard_map/up_forward/pallas_call | solution.py:42
  88.4 4.0 %down_backward.1 = (bf16[768,1536]{1,0:T(8,128)(2,1)S(1)}, bf16[768,768]{1,0:T(8,128)(2,1)S(1)}) custom-call(bf16[768,768]{1,0:T(8,128)(2,1)S(1)} %get-tuple-element.126.refs_0_, bf16[768,1536]{1,0:T(8,128)(2,1)S(1)} %bitcast.125, bf16[768,1536]{1,0:T(8,128)(2,1)S(1)} %get-tuple-element.128.refs_2_, bf16[768,1536]{1,0:T(8,128)(2,1)S(1)} %bitcast.128), custom_call_target="tpu_custom_call" | custom-call | flops 3623878656 | bytes 11796480 | tf_op jit(solution)/shard_map/down_backward/pallas_call | solution.py:42
  92.5 3.8 %down_forward.1 = (bf16[768,1536]{1,0:T(8,128)(2,1)S(1)}, bf16[768,768]{1,0:T(8,128)(2,1)S(1)}) custom-call(bf16[768,768]{1,0:T(8,128)(2,1)S(1)} %get-tuple-element.125.refs_0_, bf16[768,1536]{1,0:T(8,128)(2,1)S(1)} %get-tuple-element.129.refs_1_, bf16[768,1536]{1,0:T(8,128)(2,1)S(1)} %get-tuple-element.127.refs_7_.refs_2_, bf16[768,1536]{1,0:T(8,128)(2,1)S(1)} %bitcast.126), custom_call_target="tpu_custom_call" | custom-call | flops 3623878656 | bytes 11796480 | tf_op jit(solution)/shard_map/down_forward/pallas_call | solution.py:42
  100.9 11.7 %attention_backward.1 = (bf16[768,768]{1,0:T(8,128)(2,1)S(1)}, bf16[768,1152]{1,0:T(8,128)(2,1)S(1)}, bf16[768,768]{1,0:T(8,128)(2,1)S(1)}, f32[768,768]{1,0:T(8,128)S(1)}, f32[8,768]{1,0:T(8,128)S(1)}) custom-call(bf16[768,768]{1,0:T(8,128)(2,1)S(1)} %bitcast.91, bf16[768,768]{1,0:T(8,128)(2,1)S(1)} %mix_forward.1.refs_2_.refs_1_, ...), custom_call_target="tpu_custom_call" | custom-call | flops 2264924160 | bytes 23251968 | tf_op jit(solution)/shard_map/attention_backward/pallas_call | solution.py:42
  112.8 2.6 %projection_grads.1.refs_7_ = bf16[768,1536]{1,0:T(8,128)(2,1)S(1)} custom-call(bf16[768,768]{1,0:T(8,128)(2,1)S(1)} %get-tuple-element.139.refs_0_, bf16[768,1152]{1,0:T(8,128)(2,1)S(1)} %get-tuple-element.143.refs_1_, bf16[768,768]{1,0:T(8,128)(2,1)S(1)} %get-tuple-element.144.refs_2_, bf16[768,384]{1,0:T(8,128)(2,1)S(1)} %get-tuple-element.119.refs_0_.refs_3_), custom_call_target="tpu_custom_call" | custom-call | flops 1811939328 | bytes 7077888 | tf_op jit(solution)/shard_map/projection_grads/pallas_call | solution.py:42
  115.4 1.9 %collective-permute-done.27 = bf16[8,48,1024]{2,1,0:T(8,128)(2,1)S(1)} collective-permute-done((bf16[8,48,1024]{2,1,0:T(8,128)(2,1)S(1)}, bf16[8,48,1024]{2,1,0:T(8,128)(2,1)S(1)}, u32[]{:S(2)}, u32[]{:S(2)}) %collective-permute-start.27) | collective-permute-done | bytes 786464 | tf_op jit(solution)/shard_map/ppermute | solution.py:444
  123.3 1.7 final_forward.1
  125.0 1.9 %final_backward.1 = (bf16[768,768]{1,0:T(8,128)(2,1)S(1)}, bf16[768,128]{1,0:T(8,128)(2,1)S(1)}) custom-call(bf16[768,768]{1,0:T(8,128)(2,1)S(1)} %bitcast.93, bf16[768,768]{1,0:T(8,128)(2,1)S(1)} %bitcast.103, f32[768,768]{1,0:T(8,128)S(1)} %get-tuple-element.147.refs_2_, bf16[768,768]{1,0:T(8,128)(2,1)S(1)} %get-tuple-element.148.refs_3_, ...), custom_call_target="tpu_custom_call" | custom-call | bytes 8530944 | tf_op jit(solution)/shard_map/final_backward/pallas_call | solution.py:42
  127.8 1.7 collective-permute-start.32
  130.0 2.9 %collective-permute-done.42 = bf16[4,48,1024]{2,1,0:T(8,128)(2,1)S(1)} collective-permute-done((bf16[4,48,1024]{2,1,0:T(8,128)(2,1)S(1)}, bf16[4,48,1024]{2,1,0:T(8,128)(2,1)S(1)}, u32[]{:S(2)}, u32[]{:S(2)}) %collective-permute-start.42) | collective-permute-done | bytes 393248 | tf_op jit(solution)/shard_map/ppermute | solution.py:444
  136.3 4.8 %collective-permute-done.32 = bf16[8,48,512]{2,1,0:T(8,128)(2,1)S(1)} collective-permute-done((bf16[8,48,512]{2,1,0:T(8,128)(2,1)S(1)}, bf16[8,48,512]{2,1,0:T(8,128)(2,1)S(1)}, u32[]{:S(2)}, u32[]{:S(2)}) %collective-permute-start.32) | collective-permute-done | bytes 393248 | tf_op jit(solution)/shard_map/ppermute | solution.py:444
  142.4 5.0 %put_rows.2 = (bf16[3,2048,384]{2,1,0:T(8,128)(2,1)}, f32[8,128]{1,0:T(8,128)S(1)}) custom-call(s32[5]{0:T(128)S(1)} %pad_add_fusion.refs_0_, s32[3,256]{1,0:T(4,128)S(1)} %copy-done.5, bf16[768,768]{1,0:T(8,128)(2,1)S(1)} %get-tuple-element.146.refs_2_, bf16[3,2048,384]{2,1,0:T(8,128)(2,1)S(1)} %bitcast.105, f32[8,48,512]{2,1,0:T(8,128)S(1)} %get-tuple-element.153.refs_4_), custom_call_target="tpu_custom_call" | custom-call | flops 1207959552 | bytes 9437184 | tf_op jit(solution)/shard_map/put_rows/pallas_call | solution.py:370
  151.9 2.6 %collective-permute-done.35 = bf16[4,48,512]{2,1,0:T(8,128)(2,1)S(1)} collective-permute-done((bf16[4,48,512]{2,1,0:T(8,128)(2,1)S(1)}, bf16[4,48,512]{2,1,0:T(8,128)(2,1)S(1)}, u32[]{:S(2)}, u32[]{:S(2)}) %collective-permute-start.35) | collective-permute-done | bytes 196640 | tf_op jit(solution)/shard_map/ppermute | solution.py:444
  154.5 2.2 %collective-permute-done.36 = bf16[4,48,512]{2,1,0:T(8,128)(2,1)S(1)} collective-permute-done((bf16[4,48,512]{2,1,0:T(8,128)(2,1)S(1)}, bf16[4,48,512]{2,1,0:T(8,128)(2,1)S(1)}, u32[]{:S(2)}, u32[]{:S(2)}) %collective-permute-start.36) | collective-permute-done | bytes 196640 | tf_op jit(solution)/shard_map/ppermute | solution.py:444
  157.4 2.2 %collective-permute-start.40 = (bf16[2,48,640]{2,1,0:T(8,128)(2,1)S(1)}, bf16[2,48,640]{2,1,0:T(8,128)(2,1)S(1)}, u32[]{:S(2)}, u32[]{:S(2)}) collective-permute-start(bf16[2,48,640]{2,1,0:T(8,128)(2,1)S(1)} %get-tuple-element.174), channel_id=1, source_target_pairs={{0,8},{2,10},{4,12},{6,14},{8,0},{10,2},{12,4},{14,6},{16,24},{18,... | collective-permute-start | bytes 368648 | tf_op jit(solution)/shard_map/ppermute | solution.py:444
  161.7 2.5 %collective-permute-done.38 = bf16[2,48,512]{2,1,0:T(8,128)(2,1)S(1)} collective-permute-done((bf16[2,48,512]{2,1,0:T(8,128)(2,1)S(1)}, bf16[2,48,512]{2,1,0:T(8,128)(2,1)S(1)}, u32[]{:S(2)}, u32[]{:S(2)}) %collective-permute-start.38) | collective-permute-done | bytes 98336 | tf_op jit(solution)/shard_map/ppermute | solution.py:444
  166.4 2.2 %collective-permute-start.41 = (bf16[1,48,1664]{2,1,0:T(8,128)(2,1)S(1)}, bf16[1,48,1664]{2,1,0:T(8,128)(2,1)S(1)}, u32[]{:S(2)}, u32[]{:S(2)}) collective-permute-start(bf16[1,48,1664]{2,1,0:T(8,128)(2,1)S(1)} %get-tuple-element.176), channel_id=1, source_target_pairs={{0,16},{2,18},{4,20},{6,22},{8,24},{10,26},{12,28},{14,30},{16,0},... | collective-permute-start | bytes 479240 | tf_op jit(solution)/shard_map/ppermute | solution.py:444
  170.0 5.0 %put_rows.3 = (bf16[3,2048,384]{2,1,0:T(8,128)(2,1)}, f32[8,128]{1,0:T(8,128)}) custom-call(s32[5]{0:T(128)S(1)} %pad_add_fusion.refs_0_, s32[3,256]{1,0:T(4,128)S(1)} %copy-done.5, bf16[768,768]{1,0:T(8,128)(2,1)S(1)} %get-tuple-element.155.refs_2_, bf16[3,2048,384]{2,1,0:T(8,128)(2,1)S(1)} %bitcast.107, f32[8,128]{1,0:T(8,128)S(1)} %get-tuple-element.156.refs_4_.refs_7_), custom_call_target="tpu_custom_call" | custom-call | flops 1207959552 | bytes 9437184 | tf_op jit(solution)/shard_map/put_rows/pallas_call | solution.py:370
  (150 shorter events, 59.6 us)
Async XLA Ops:
  3.1 12.7 %collective-permute-start = (bf16[1,48,1664]{2,1,0:T(8,128)(2,1)S(1)}, bf16[1,48,1664]{2,1,0:T(8,128)(2,1)S(1)}, u32[]{:S(2)}, u32[]{:S(2)}) collective-permute-start(bf16[1,48,1664]{2,1,0:T(8,128)(2,1)S(1)} %bitcast.149), channel_id=1, source_target_pairs={{0,16},{2,18},{4,20},{6,22},{8,24},{10,26},{12,28},{14,30},{16,0},... | collective-permute-start | bytes 479240 | tf_op jit(solution)/shard_map/ppermute | solution.py:444
  21.5 15.6 %collective-permute-start.5 = (bf16[1,48,3072]{2,1,0:T(8,128)(2,1)S(1)}, bf16[1,48,3072]{2,1,0:T(8,128)(2,1)S(1)}, u32[]{:S(2)}, u32[]{:S(2)}) collective-permute-start(bf16[1,48,3072]{2,1,0:T(8,128)(2,1)S(1)} %bitcast.123), channel_id=1, source_target_pairs={{0,16},{2,18},{4,20},{6,22},{8,24},{10,26},{12,28},{14,30},{16,0},... | collective-permute-start | bytes 884744 | tf_op jit(solution)/shard_map/ppermute | solution.py:444
  25.3 12.2 %collective-permute-start.7 = (bf16[4,48,640]{2,1,0:T(8,128)(2,1)S(1)}, bf16[4,48,640]{2,1,0:T(8,128)(2,1)S(1)}, u32[]{:S(2)}, u32[]{:S(2)}) collective-permute-start(bf16[4,48,640]{2,1,0:T(8,128)(2,1)S(1)} %bitcast.168), channel_id=1, source_target_pairs={{0,8},{2,10},{4,12},{6,14},{8,0},{10,2},{12,4},{14,6},{16,24},{18,... | collective-permute-start | bytes 737288 | tf_op jit(solution)/shard_map/ppermute | solution.py:444
  27.8 9.3 %collective-permute-start.6 = (bf16[4,48,512]{2,1,0:T(8,128)(2,1)S(1)}, bf16[4,48,512]{2,1,0:T(8,128)(2,1)S(1)}, u32[]{:S(2)}, u32[]{:S(2)}) collective-permute-start(bf16[4,48,512]{2,1,0:T(8,128)(2,1)S(1)} %bitcast.137), channel_id=1, source_target_pairs={{0,4},{2,6},{4,0},{6,2},{8,12},{10,14},{12,8},{14,10},{16,20},{18,... | collective-permute-start | bytes 589832 | tf_op jit(solution)/shard_map/ppermute | solution.py:444
  28.3 8.8 %collective-permute-start.8 = (bf16[4,48,512]{2,1,0:T(8,128)(2,1)S(1)}, bf16[4,48,512]{2,1,0:T(8,128)(2,1)S(1)}, u32[]{:S(2)}, u32[]{:S(2)}) collective-permute-start(bf16[4,48,512]{2,1,0:T(8,128)(2,1)S(1)} %bitcast.173), channel_id=1, source_target_pairs={{0,2},{2,0},{4,6},{6,4},{8,10},{10,8},{12,14},{14,12},{16,18},{18,... | collective-permute-start | bytes 589832 | tf_op jit(solution)/shard_map/ppermute | solution.py:444
  38.1 12.0 %collective-permute-start.12 = (bf16[8,48,512]{2,1,0:T(8,128)(2,1)S(1)}, bf16[8,48,512]{2,1,0:T(8,128)(2,1)S(1)}, u32[]{:S(2)}, u32[]{:S(2)}) collective-permute-start(bf16[8,48,512]{2,1,0:T(8,128)(2,1)S(1)} %bitcast.132), channel_id=1, source_target_pairs={{0,8},{2,10},{4,12},{6,14},{8,0},{10,2},{12,4},{14,6},{16,24},{18,... | collective-permute-start | bytes 1179656 | tf_op jit(solution)/shard_map/ppermute | solution.py:444
  38.3 13.6 %collective-permute-start.13 = (bf16[8,48,640]{2,1,0:T(8,128)(2,1)S(1)}, bf16[8,48,640]{2,1,0:T(8,128)(2,1)S(1)}, u32[]{:S(2)}, u32[]{:S(2)}) collective-permute-start(bf16[8,48,640]{2,1,0:T(8,128)(2,1)S(1)} %bitcast.153), channel_id=1, source_target_pairs={{0,2},{2,0},{4,6},{6,4},{8,10},{10,8},{12,14},{14,12},{16,18},{18,... | collective-permute-start | bytes 1474568 | tf_op jit(solution)/shard_map/ppermute | solution.py:444
  38.8 11.8 %collective-permute-start.14 = (bf16[8,48,512]{2,1,0:T(8,128)(2,1)S(1)}, bf16[8,48,512]{2,1,0:T(8,128)(2,1)S(1)}, u32[]{:S(2)}, u32[]{:S(2)}) collective-permute-start(bf16[8,48,512]{2,1,0:T(8,128)(2,1)S(1)} %bitcast.165), channel_id=1, source_target_pairs={{0,4},{2,6},{4,0},{6,2},{8,12},{10,14},{12,8},{14,10},{16,20},{18,... | collective-permute-start | bytes 1179656 | tf_op jit(solution)/shard_map/ppermute | solution.py:444
  40.2 12.4 %collective-permute-start.10 = (bf16[2,48,1024]{2,1,0:T(8,128)(2,1)S(1)}, bf16[2,48,1024]{2,1,0:T(8,128)(2,1)S(1)}, u32[]{:S(2)}, u32[]{:S(2)}) collective-permute-start(bf16[2,48,1024]{2,1,0:T(8,128)(2,1)S(1)} %get-tuple-element.111.refs_3_), channel_id=1, source_target_pairs={{0,4},{2,6},{4,0},{6,2},{8,12},{10,14},{12,8},{14,10},{16,20},{18,... | collective-permute-start | bytes 589832 | tf_op jit(solution)/shard_map/ppermute | solution.py:444
  41.6 11.0 %collective-permute-start.11 = (bf16[2,48,1024]{2,1,0:T(8,128)(2,1)S(1)}, bf16[2,48,1024]{2,1,0:T(8,128)(2,1)S(1)}, u32[]{:S(2)}, u32[]{:S(2)}) collective-permute-start(bf16[2,48,1024]{2,1,0:T(8,128)(2,1)S(1)} %get-tuple-element.112.refs_5_), channel_id=1, source_target_pairs={{0,8},{2,10},{4,12},{6,14},{8,0},{10,2},{12,4},{14,6},{16,24},{18,... | collective-permute-start | bytes 589832 | tf_op jit(solution)/shard_map/ppermute | solution.py:444
  63.5 17.5 %collective-permute-start.16 = (bf16[768,768]{1,0:T(8,128)(2,1)S(1)}, bf16[768,768]{1,0:T(8,128)(2,1)S(1)}, u32[]{:S(2)}, u32[]{:S(2)}) collective-permute-start(bf16[768,768]{1,0:T(8,128)(2,1)S(1)} %mix_forward.1.refs_2_.refs_1_), channel_id=1, source_target_pairs={{0,1},{1,0},{2,3},{3,2},{4,5},{5,4},{6,7},{7,6},{8,9},{9,8},{10,11... | collective-permute-start | bytes 3538952 | tf_op jit(solution)/shard_map/ppermute | solution.py:598
  65.9 12.1 %collective-permute-start.20 = (bf16[8,48,512]{2,1,0:T(8,128)(2,1)S(1)}, bf16[8,48,512]{2,1,0:T(8,128)(2,1)S(1)}, u32[]{:S(2)}, u32[]{:S(2)}) collective-permute-start(bf16[8,48,512]{2,1,0:T(8,128)(2,1)S(1)} %get-tuple-element.204.refs_1_), channel_id=1, source_target_pairs={{0,8},{2,10},{4,12},{6,14},{8,0},{10,2},{12,4},{14,6},{16,24},{18,... | collective-permute-start | bytes 1179656 | tf_op jit(solution)/shard_map/ppermute | solution.py:444
  67.7 10.8 %collective-permute-start.21 = (bf16[8,48,512]{2,1,0:T(8,128)(2,1)S(1)}, bf16[8,48,512]{2,1,0:T(8,128)(2,1)S(1)}, u32[]{:S(2)}, u32[]{:S(2)}) collective-permute-start(bf16[8,48,512]{2,1,0:T(8,128)(2,1)S(1)} %get-tuple-element.202.refs_3_), channel_id=1, source_target_pairs={{0,2},{2,0},{4,6},{6,4},{8,10},{10,8},{12,14},{14,12},{16,18},{18,... | collective-permute-start | bytes 1179656 | tf_op jit(solution)/shard_map/ppermute | solution.py:444
  68.4 11.9 %collective-permute-start.22 = (bf16[8,48,512]{2,1,0:T(8,128)(2,1)S(1)}, bf16[8,48,512]{2,1,0:T(8,128)(2,1)S(1)}, u32[]{:S(2)}, u32[]{:S(2)}) collective-permute-start(bf16[8,48,512]{2,1,0:T(8,128)(2,1)S(1)} %get-tuple-element.200.refs_5_), channel_id=1, source_target_pairs={{0,4},{2,6},{4,0},{6,2},{8,12},{10,14},{12,8},{14,10},{16,20},{18,... | collective-permute-start | bytes 1179656 | tf_op jit(solution)/shard_map/ppermute | solution.py:444
  69.9 17.8 %collective-permute-start.23 = (bf16[8,48,512]{2,1,0:T(8,128)(2,1)S(1)}, bf16[8,48,512]{2,1,0:T(8,128)(2,1)S(1)}, u32[]{:S(2)}, u32[]{:S(2)}) collective-permute-start(bf16[8,48,512]{2,1,0:T(8,128)(2,1)S(1)} %get-tuple-element.203.refs_1_), channel_id=1, source_target_pairs={{0,8},{2,10},{4,12},{6,14},{8,0},{10,2},{12,4},{14,6},{16,24},{18,... | collective-permute-start | bytes 1179656 | tf_op jit(solution)/shard_map/ppermute | solution.py:444
  78.0 9.7 %collective-permute-start.24 = (bf16[8,48,512]{2,1,0:T(8,128)(2,1)S(1)}, bf16[8,48,512]{2,1,0:T(8,128)(2,1)S(1)}, u32[]{:S(2)}, u32[]{:S(2)}) collective-permute-start(bf16[8,48,512]{2,1,0:T(8,128)(2,1)S(1)} %get-tuple-element.201.refs_3_), channel_id=1, source_target_pairs={{0,2},{2,0},{4,6},{6,4},{8,10},{10,8},{12,14},{14,12},{16,18},{18,... | collective-permute-start | bytes 1179656 | tf_op jit(solution)/shard_map/ppermute | solution.py:444
  78.5 9.2 %collective-permute-start.25 = (bf16[8,48,512]{2,1,0:T(8,128)(2,1)S(1)}, bf16[8,48,512]{2,1,0:T(8,128)(2,1)S(1)}, u32[]{:S(2)}, u32[]{:S(2)}) collective-permute-start(bf16[8,48,512]{2,1,0:T(8,128)(2,1)S(1)} %get-tuple-element.199.refs_5_), channel_id=1, source_target_pairs={{0,4},{2,6},{4,0},{6,2},{8,12},{10,14},{12,8},{14,10},{16,20},{18,... | collective-permute-start | bytes 1179656 | tf_op jit(solution)/shard_map/ppermute | solution.py:444
  97.3 20.0 %collective-permute-start.27 = (bf16[8,48,1024]{2,1,0:T(8,128)(2,1)S(1)}, bf16[8,48,1024]{2,1,0:T(8,128)(2,1)S(1)}, u32[]{:S(2)}, u32[]{:S(2)}) collective-permute-start(bf16[8,48,1024]{2,1,0:T(8,128)(2,1)S(1)} %get-tuple-element.134), channel_id=1, source_target_pairs={{0,8},{2,10},{4,12},{6,14},{8,0},{10,2},{12,4},{14,6},{16,24},{18,... | collective-permute-start | bytes 2359304 | tf_op jit(solution)/shard_map/ppermute | solution.py:444
  98.9 19.7 %collective-permute-start.28 = (bf16[8,48,1024]{2,1,0:T(8,128)(2,1)S(1)}, bf16[8,48,1024]{2,1,0:T(8,128)(2,1)S(1)}, u32[]{:S(2)}, u32[]{:S(2)}) collective-permute-start(bf16[8,48,1024]{2,1,0:T(8,128)(2,1)S(1)} %get-tuple-element.136), channel_id=1, source_target_pairs={{0,2},{2,0},{4,6},{6,4},{8,10},{10,8},{12,14},{14,12},{16,18},{18,... | collective-permute-start | bytes 2359304 | tf_op jit(solution)/shard_map/ppermute | solution.py:444
  100.4 19.4 %collective-permute-start.29 = (bf16[8,48,1024]{2,1,0:T(8,128)(2,1)S(1)}, bf16[8,48,1024]{2,1,0:T(8,128)(2,1)S(1)}, u32[]{:S(2)}, u32[]{:S(2)}) collective-permute-start(bf16[8,48,1024]{2,1,0:T(8,128)(2,1)S(1)} %get-tuple-element.138), channel_id=1, source_target_pairs={{0,4},{2,6},{4,0},{6,2},{8,12},{10,14},{12,8},{14,10},{16,20},{18,... | collective-permute-start | bytes 2359304 | tf_op jit(solution)/shard_map/ppermute | solution.py:444
  100.9 22.4 %collective-permute-start.26 = (bf16[768,768]{1,0:T(8,128)(2,1)S(1)}, bf16[768,768]{1,0:T(8,128)(2,1)S(1)}, u32[]{:S(2)}, u32[]{:S(2)}) collective-permute-start(bf16[768,768]{1,0:T(8,128)(2,1)S(1)} %get-tuple-element.130.refs_1_.refs_4_), channel_id=1, source_target_pairs={{0,1},{1,0},{2,3},{3,2},{4,5},{5,4},{6,7},{7,6},{8,9},{9,8},{10,11... | collective-permute-start | bytes 3538952 | tf_op jit(solution)/shard_map/ppermute | solution.py:598
  120.9 12.0 %collective-permute-start.42 = (bf16[4,48,1024]{2,1,0:T(8,128)(2,1)S(1)}, bf16[4,48,1024]{2,1,0:T(8,128)(2,1)S(1)}, u32[]{:S(2)}, u32[]{:S(2)}) collective-permute-start(bf16[4,48,1024]{2,1,0:T(8,128)(2,1)S(1)} %get-tuple-element.179), channel_id=1, source_target_pairs={{0,4},{2,6},{4,0},{6,2},{8,12},{10,14},{12,8},{14,10},{16,20},{18,... | collective-permute-start | bytes 1179656 | tf_op jit(solution)/shard_map/ppermute | solution.py:444
  121.5 12.0 %collective-permute-start.43 = (bf16[4,48,1024]{2,1,0:T(8,128)(2,1)S(1)}, bf16[4,48,1024]{2,1,0:T(8,128)(2,1)S(1)}, u32[]{:S(2)}, u32[]{:S(2)}) collective-permute-start(bf16[4,48,1024]{2,1,0:T(8,128)(2,1)S(1)} %get-tuple-element.181), channel_id=1, source_target_pairs={{0,8},{2,10},{4,12},{6,14},{8,0},{10,2},{12,4},{14,6},{16,24},{18,... | collective-permute-start | bytes 1179656 | tf_op jit(solution)/shard_map/ppermute | solution.py:444
  122.8 10.9 %collective-permute-start.44 = (bf16[4,48,1024]{2,1,0:T(8,128)(2,1)S(1)}, bf16[4,48,1024]{2,1,0:T(8,128)(2,1)S(1)}, u32[]{:S(2)}, u32[]{:S(2)}) collective-permute-start(bf16[4,48,1024]{2,1,0:T(8,128)(2,1)S(1)} %get-tuple-element.183), channel_id=1, source_target_pairs={{0,2},{2,0},{4,6},{6,4},{8,10},{10,8},{12,14},{14,12},{16,18},{18,... | collective-permute-start | bytes 1179656 | tf_op jit(solution)/shard_map/ppermute | solution.py:444
  127.8 13.3 %collective-permute-start.32 = (bf16[8,48,512]{2,1,0:T(8,128)(2,1)S(1)}, bf16[8,48,512]{2,1,0:T(8,128)(2,1)S(1)}, u32[]{:S(2)}, u32[]{:S(2)}) collective-permute-start(bf16[8,48,512]{2,1,0:T(8,128)(2,1)S(1)} %get-tuple-element.158), channel_id=1, source_target_pairs={{0,8},{2,10},{4,12},{6,14},{8,0},{10,2},{12,4},{14,6},{16,24},{18,... | collective-permute-start | bytes 1179656 | tf_op jit(solution)/shard_map/ppermute | solution.py:444
  129.5 17.9 %collective-permute-start.34 = (bf16[8,48,640]{2,1,0:T(8,128)(2,1)S(1)}, bf16[8,48,640]{2,1,0:T(8,128)(2,1)S(1)}, u32[]{:S(2)}, u32[]{:S(2)}) collective-permute-start(bf16[8,48,640]{2,1,0:T(8,128)(2,1)S(1)} %get-tuple-element.162), channel_id=1, source_target_pairs={{0,4},{2,6},{4,0},{6,2},{8,12},{10,14},{12,8},{14,10},{16,20},{18,... | collective-permute-start | bytes 1474568 | tf_op jit(solution)/shard_map/ppermute | solution.py:444
  132.9 14.5 %collective-permute-start.33 = (bf16[8,48,512]{2,1,0:T(8,128)(2,1)S(1)}, bf16[8,48,512]{2,1,0:T(8,128)(2,1)S(1)}, u32[]{:S(2)}, u32[]{:S(2)}) collective-permute-start(bf16[8,48,512]{2,1,0:T(8,128)(2,1)S(1)} %get-tuple-element.160), channel_id=1, source_target_pairs={{0,2},{2,0},{4,6},{6,4},{8,10},{10,8},{12,14},{14,12},{16,18},{18,... | collective-permute-start | bytes 1179656 | tf_op jit(solution)/shard_map/ppermute | solution.py:444
  134.5 15.1 %collective-permute-start.45 = (bf16[2,48,1024]{2,1,0:T(8,128)(2,1)S(1)}, bf16[2,48,1024]{2,1,0:T(8,128)(2,1)S(1)}, u32[]{:S(2)}, u32[]{:S(2)}) collective-permute-start(bf16[2,48,1024]{2,1,0:T(8,128)(2,1)S(1)} %get-tuple-element.185), channel_id=1, source_target_pairs={{0,2},{2,0},{4,6},{6,4},{8,10},{10,8},{12,14},{14,12},{16,18},{18,... | collective-permute-start | bytes 589832 | tf_op jit(solution)/shard_map/ppermute | solution.py:444
  135.8 15.2 %collective-permute-start.46 = (bf16[2,48,1024]{2,1,0:T(8,128)(2,1)S(1)}, bf16[2,48,1024]{2,1,0:T(8,128)(2,1)S(1)}, u32[]{:S(2)}, u32[]{:S(2)}) collective-permute-start(bf16[2,48,1024]{2,1,0:T(8,128)(2,1)S(1)} %get-tuple-element.187), channel_id=1, source_target_pairs={{0,4},{2,6},{4,0},{6,2},{8,12},{10,14},{12,8},{14,10},{16,20},{18,... | collective-permute-start | bytes 589832 | tf_op jit(solution)/shard_map/ppermute | solution.py:444
  141.1 9.9 %collective-permute-start.47 = (bf16[2,48,1024]{2,1,0:T(8,128)(2,1)S(1)}, bf16[2,48,1024]{2,1,0:T(8,128)(2,1)S(1)}, u32[]{:S(2)}, u32[]{:S(2)}) collective-permute-start(bf16[2,48,1024]{2,1,0:T(8,128)(2,1)S(1)} %get-tuple-element.189), channel_id=1, source_target_pairs={{0,8},{2,10},{4,12},{6,14},{8,0},{10,2},{12,4},{14,6},{16,24},{18,... | collective-permute-start | bytes 589832 | tf_op jit(solution)/shard_map/ppermute | solution.py:444
  151.7 17.4 %collective-permute-start.48 = (bf16[1,48,3072]{2,1,0:T(8,128)(2,1)S(1)}, bf16[1,48,3072]{2,1,0:T(8,128)(2,1)S(1)}, u32[]{:S(2)}, u32[]{:S(2)}) collective-permute-start(bf16[1,48,3072]{2,1,0:T(8,128)(2,1)S(1)} %get-tuple-element.191), channel_id=1, source_target_pairs={{0,16},{2,18},{4,20},{6,22},{8,24},{10,26},{12,28},{14,30},{16,0},... | collective-permute-start | bytes 884744 | tf_op jit(solution)/shard_map/ppermute | solution.py:444
  166.4 8.6 %collective-permute-start.41 = (bf16[1,48,1664]{2,1,0:T(8,128)(2,1)S(1)}, bf16[1,48,1664]{2,1,0:T(8,128)(2,1)S(1)}, u32[]{:S(2)}, u32[]{:S(2)}) collective-permute-start(bf16[1,48,1664]{2,1,0:T(8,128)(2,1)S(1)} %get-tuple-element.176), channel_id=1, source_target_pairs={{0,16},{2,18},{4,20},{6,22},{8,24},{10,26},{12,28},{14,30},{16,0},... | collective-permute-start | bytes 479240 | tf_op jit(solution)/shard_map/ppermute | solution.py:444
  (30 other events, 186.7 us)
where the time goes:
time: 177 us; the launch traced here: 176 us
  Pallas kernels  68.7 us (39%)
  starting transfers between devices  48.9 us (28%)
  waiting for transfers between devices  47.8 us (27%)
  local copies, waits for them, and re-layouts  7.44 us (4%)
  other arithmetic  2.26 us (1%)
    pallas_call x32, Pallas kernels, call(): pl.pallas_call(body, out_shape=outs, in_specs=[pl.BlockSpec(memory_space=...  51.9 us
    ppermute x43, starting transfers between devices, swap(): lax.ppermute(value, 'dp', [(i, i ^ 1 << bit) for i in range(self.count)])  48.1 us
    ppermute x43, waiting for transfers between devices, swap(): lax.ppermute(value, 'dp', [(i, i ^ 1 << bit) for i in range(self.count)])  47.8 us
    pallas_call x2, Pallas kernels, put(): pl.pallas_call(body, grid=(rows, length // long), out_shape=(shape(base.s...  10 us
    pallas_call x2, Pallas kernels, select(): pl.pallas_call(body, grid=(rows,), out_shape=outs if mask else outs[:1],...  6.8 us
    unnamed x27, local copies, waits for them, and re-layouts  6.56 us
  transfers between devices with their start and end apart: 49, of which 22 were waited for; matrix products, arithmetic and copies ran while one was open for 1% of the time, Pallas kernels for 35%

commit v1 on v0

--- a/solution.py
+++ b/solution.py
@@ -775,15 +775,15 @@
         flops=8 * token_count * width * half_width,
         name="projection_grads",
     )
-    both_grads = fold(cube, alone(both_grads), back_bits(1), [first_grad])
-    pre_other = other_core(tie(pre_own, both_grads[0].value))
     finished, logit_grad, router_grad = call(
         functools.partial(final_forward, *by_row),
         (wide, shape((token_count, 1), F32), vector),
         (states, upstream, att_own, att_other, feed_own, feed_other, gains, keep),
-        after=[both_grads[0].value],
+        after=[first_grad],
         name="final_forward",
     )
+    both_grads = fold(cube, alone(both_grads), back_bits(1), [logit_grad])
+    pre_other = other_core(tie(pre_own, both_grads[0].value))
     total_grad, vector_grads = call(
         functools.partial(final_backward, *by_row),
         (wide, shape((width, 128))),
@@ -794,15 +794,18 @@
     first_grads = alone(cut(cube, first_grad))
     first_grads[-1] += cut(cube, vector_grads)
     first_grads = fold(cube, first_grads, back_bits(0))
-    result, done = put(tokens, chosen, finished, cube.bits, [first_grads[0].value])
+    for step in range(2, steps):
+        both_grads = fold(cube, alone(both_grads), back_bits(step), [first_grad] if step == 2 else [])
+    first_grads = fold(cube, alone(first_grads), back_bits(1))
+    both_grads = [both_grads]
+    for bit in cube.far:
+        both_grads = [fold(cube, both_grads, [bit])]
+    result, done = put(tokens, chosen, finished, cube.bits, [both_grads[0][0].value])
     tokens_grad, _ = put(cotangent, chosen, total_grad, cube.bits, [done])
     for step in range(2, steps):
-        both_grads = fold(cube, alone(both_grads), back_bits(step), [first_grad] if step == 2 else [])
-    for step in range(1, steps):
-        first_grads = fold(cube, alone(first_grads), back_bits(step), [done] if step == 1 else [])
-    both_grads, first_grads = [both_grads], [first_grads]
+        first_grads = fold(cube, alone(first_grads), back_bits(step), [done] if step == 2 else [])
+    first_grads = [first_grads]
     for bit in cube.far:
-        both_grads = [fold(cube, both_grads, [bit])]
         first_grads = [fold(cube, first_grads, [bit])]
     (both_grad,), (first_grad,) = both_grads[0], first_grads[0]
     up_out, down_out = call(

time: 177 us -> 175 us (0.989)
  starting transfers between devices: 48.9 us -> 46 us
    ppermute x43, starting transfers between devices: 48.1 us -> 44.6 us  [swap(): lax.ppermute(value, 'dp', [(i, i ^ 1 << bit) for i in range(self.count)])]
  transfers between devices with their start and end apart: 49 -> 49, of which waited for: 22 -> 24; matrix products, arithmetic and copies ran while one was open for 1% -> 1% of each run, Pallas kernels for 35% -> 35%
where the time goes in v1:
time: 175 us; the launch traced here: 174 us
  Pallas kernels  68.5 us (39%)
  waiting for transfers between devices  49 us (28%)
  starting transfers between devices  46 us (26%)
  local copies, waits for them, and re-layouts  7.47 us (4%)
  other arithmetic  2.26 us (1%)
    pallas_call x32, Pallas kernels, call(): pl.pallas_call(body, out_shape=outs, in_specs=[pl.BlockSpec(memory_space=...  51.7 us
    ppermute x43, waiting for transfers between devices, swap(): lax.ppermute(value, 'dp', [(i, i ^ 1 << bit) for i in range(self.count)])  48.4 us
    ppermute x43, starting transfers between devices, swap(): lax.ppermute(value, 'dp', [(i, i ^ 1 << bit) for i in range(self.count)])  44.6 us
    pallas_call x2, Pallas kernels, put(): pl.pallas_call(body, grid=(rows, length // long), out_shape=(shape(base.s...  10 us
    pallas_call x2, Pallas kernels, select(): pl.pallas_call(body, grid=(rows,), out_shape=outs if mask else outs[:1],...  6.8 us
    unnamed x27, local copies, waits for them, and re-layouts  6.55 us
  transfers between devices with their start and end apart: 49, of which 24 were waited for; matrix products, arithmetic and copies ran while one was open for 1% of the time, Pallas kernels for 35%

profile of v1, /device:TPU:0, one launch (start us, length us, event | category | flops | bytes accessed | tf_op | source)
XLA Modules:
  0.0 174.3 jit_solution(9890671726916390737)
XLA Ops:
  3.1 4.1 %collective-permute-start = (bf16[1,48,1664]{2,1,0:T(8,128)(2,1)S(1)}, bf16[1,48,1664]{2,1,0:T(8,128)(2,1)S(1)}, u32[]{:S(2)}, u32[]{:S(2)}) collective-permute-start(bf16[1,48,1664]{2,1,0:T(8,128)(2,1)S(1)} %bitcast.149), channel_id=1, source_target_pairs={{0,16},{2,18},{4,20},{6,22},{8,24},{10,26},{12,28},{14,30},{16,0},... | collective-permute-start | bytes 479240 | tf_op jit(solution)/shard_map/ppermute | solution.py:444
  7.3 2.3 %copy-done = bf16[3,2048,384]{2,1,0:T(8,128)(2,1)S(1)} copy-done((bf16[3,2048,384]{2,1,0:T(8,128)(2,1)S(1)}, bf16[3,2048,384]{2,1,0:T(8,128)(2,1)}, u32[]{:S(2)}) %copy-start) | copy-done | bytes 4718616
  11.9 3.9 %select_rows.2 = (bf16[3,256,384]{2,1,0:T(8,128)(2,1)S(1)}, f32[3,256,256]{2,1,0:T(8,128)S(1)}, f32[768,1]{1,0:T(8,128)S(1)}) custom-call(bf16[3,2048,384]{2,1,0:T(8,128)(2,1)S(1)} %copy-done, s32[3,256]{1,0:T(4,128)S(1)} %copy-done.4, s32[3,2048]{1,0:T(4,128)S(1)} %copy-done.7, s32[3,2048]{1,0:T(4,128)S(1)} %copy-done.8), custom_call_target="tpu_custom_call" | custom-call | flops 1207959552 | bytes 4718592 | tf_op jit(solution)/shard_map/select_rows/pallas_call | solution.py:329
  16.8 1.6 collective-permute-start.2
  19.9 1.6 collective-permute-start.4
  25.3 2.5 %collective-permute-start.7 = (bf16[4,48,640]{2,1,0:T(8,128)(2,1)S(1)}, bf16[4,48,640]{2,1,0:T(8,128)(2,1)S(1)}, u32[]{:S(2)}, u32[]{:S(2)}) collective-permute-start(bf16[4,48,640]{2,1,0:T(8,128)(2,1)S(1)} %bitcast.168), channel_id=1, source_target_pairs={{0,8},{2,10},{4,12},{6,14},{8,0},{10,2},{12,4},{14,6},{16,24},{18,... | collective-permute-start | bytes 737288 | tf_op jit(solution)/shard_map/ppermute | solution.py:444
  28.9 2.9 %select_rows.3.refs_8_.refs_0_ = bf16[3,256,384]{2,1,0:T(8,128)(2,1)S(1)} custom-call(bf16[3,2048,384]{2,1,0:T(8,128)(2,1)S(1)} %bitcast.107, s32[3,256]{1,0:T(4,128)S(1)} %copy-done.5, bf16[4,48,512]{2,1,0:T(8,128)(2,1)S(1)} %bitcast.137), custom_call_target="tpu_custom_call" | custom-call | flops 1207959552 | bytes 4718592 | tf_op jit(solution)/shard_map/select_rows/pallas_call | solution.py:329
  31.7 5.3 %collective-permute-done.5.refs_2_.refs_7_ = bf16[1,48,3072]{2,1,0:T(8,128)(2,1)S(1)} collective-permute-done((bf16[1,48,3072]{2,1,0:T(8,128)(2,1)S(1)}, bf16[1,48,3072]{2,1,0:T(8,128)(2,1)S(1)}, u32[]{:S(2)}, u32[]{:S(2)}) %collective-permute-start.5) | collective-permute-done | bytes 294944 | tf_op jit(solution)/shard_map/ppermute | solution.py:444
  41.6 1.9 %collective-permute-start.11 = (bf16[2,48,1024]{2,1,0:T(8,128)(2,1)S(1)}, bf16[2,48,1024]{2,1,0:T(8,128)(2,1)S(1)}, u32[]{:S(2)}, u32[]{:S(2)}) collective-permute-start(bf16[2,48,1024]{2,1,0:T(8,128)(2,1)S(1)} %get-tuple-element.112.refs_5_), channel_id=1, source_target_pairs={{0,8},{2,10},{4,12},{6,14},{8,0},{10,2},{12,4},{14,6},{16,24},{18,... | collective-permute-start | bytes 589832 | tf_op jit(solution)/shard_map/ppermute | solution.py:444
  43.5 6.6 %collective-permute-done.12.refs_2_ = bf16[8,48,512]{2,1,0:T(8,128)(2,1)S(1)} collective-permute-done((bf16[8,48,512]{2,1,0:T(8,128)(2,1)S(1)}, bf16[8,48,512]{2,1,0:T(8,128)(2,1)S(1)}, u32[]{:S(2)}, u32[]{:S(2)}) %collective-permute-start.12) | collective-permute-done | bytes 393248 | tf_op jit(solution)/shard_map/ppermute | solution.py:444
  52.6 3.2 %collective-permute-done.9.refs_2_ = bf16[2,48,1024]{2,1,0:T(8,128)(2,1)S(1)} collective-permute-done((bf16[2,48,1024]{2,1,0:T(8,128)(2,1)S(1)}, bf16[2,48,1024]{2,1,0:T(8,128)(2,1)S(1)}, u32[]{:S(2)}, u32[]{:S(2)}) %collective-permute-start.9) | collective-permute-done | bytes 196640 | tf_op jit(solution)/shard_map/ppermute | solution.py:444
  57.9 4.7 %attention_forward.1 = (bf16[768,768]{1,0:T(8,128)(2,1)S(1)}, bf16[768,1152]{1,0:T(8,128)(2,1)S(1)}, f32[3,6,256,256]{3,2,1,0:T(8,128)S(1)}, bf16[768,384]{1,0:T(8,128)(2,1)S(1)}, f32[8,768]{1,0:T(8,128)S(1)}) custom-call(bf16[768,768]{1,0:T(8,128)(2,1)S(1)} %bitcast.89, bf16[768,1664]{1,0:T(8,128)(2,1)S(1)} %bitcast.86, ...), custom_call_target="tpu_custom_call" | custom-call | flops 1358954496 | bytes 12804096 | tf_op jit(solution)/shard_map/attention_forward/pallas_call | solution.py:42
  65.9 1.7 collective-permute-start.20
  68.4 1.6 collective-permute-start.22
  70.6 7.4 %collective-permute-done.20.refs_2_ = bf16[8,48,512]{2,1,0:T(8,128)(2,1)S(1)} collective-permute-done((bf16[8,48,512]{2,1,0:T(8,128)(2,1)S(1)}, bf16[8,48,512]{2,1,0:T(8,128)(2,1)S(1)}, u32[]{:S(2)}, u32[]{:S(2)}) %collective-permute-start.20) | collective-permute-done | bytes 393248 | tf_op jit(solution)/shard_map/ppermute | solution.py:444
  78.5 1.7 collective-permute-start.25
  81.0 6.6 %up_forward.1 = (bf16[768,768]{1,0:T(8,128)(2,1)S(1)}, bf16[768,1536]{1,0:T(8,128)(2,1)S(1)}, bf16[768,1536]{1,0:T(8,128)(2,1)S(1)}, bf16[768,768]{1,0:T(8,128)(2,1)S(1)}, bf16[768,1536]{1,0:T(8,128)(2,1)S(1)}) custom-call(bf16[768,768]{1,0:T(8,128)(2,1)S(1)} %bitcast.90, bf16[768,768]{1,0:T(8,128)(2,1)S(1)} %bitcast.100, ...), custom_call_target="tpu_custom_call" | custom-call | flops 3623878656 | bytes 16542720 | tf_op jit(solution)/shard_map/up_forward/pallas_call | solution.py:42
  88.4 3.9 %down_backward.1 = (bf16[768,1536]{1,0:T(8,128)(2,1)S(1)}, bf16[768,768]{1,0:T(8,128)(2,1)S(1)}) custom-call(bf16[768,768]{1,0:T(8,128)(2,1)S(1)} %get-tuple-element.126.refs_0_, bf16[768,1536]{1,0:T(8,128)(2,1)S(1)} %bitcast.124, bf16[768,1536]{1,0:T(8,128)(2,1)S(1)} %get-tuple-element.128.refs_2_, bf16[768,1536]{1,0:T(8,128)(2,1)S(1)} %bitcast.127), custom_call_target="tpu_custom_call" | custom-call | flops 3623878656 | bytes 11796480 | tf_op jit(solution)/shard_map/down_backward/pallas_call | solution.py:42
  92.5 3.8 %down_forward.1 = (bf16[768,1536]{1,0:T(8,128)(2,1)S(1)}, bf16[768,768]{1,0:T(8,128)(2,1)S(1)}) custom-call(bf16[768,768]{1,0:T(8,128)(2,1)S(1)} %get-tuple-element.125.refs_0_, bf16[768,1536]{1,0:T(8,128)(2,1)S(1)} %get-tuple-element.129.refs_1_, bf16[768,1536]{1,0:T(8,128)(2,1)S(1)} %get-tuple-element.127.refs_7_.refs_2_, bf16[768,1536]{1,0:T(8,128)(2,1)S(1)} %bitcast.125), custom_call_target="tpu_custom_call" | custom-call | flops 3623878656 | bytes 11796480 | tf_op jit(solution)/shard_map/down_forward/pallas_call | solution.py:42
  97.9 1.5 collective-permute-start.28
  99.4 1.6 collective-permute-start.29
  101.5 11.7 %attention_backward.1 = (bf16[768,768]{1,0:T(8,128)(2,1)S(1)}, bf16[768,1152]{1,0:T(8,128)(2,1)S(1)}, bf16[768,768]{1,0:T(8,128)(2,1)S(1)}, f32[768,768]{1,0:T(8,128)S(1)}, f32[8,768]{1,0:T(8,128)S(1)}) custom-call(bf16[768,768]{1,0:T(8,128)(2,1)S(1)} %bitcast.91, bf16[768,768]{1,0:T(8,128)(2,1)S(1)} %mix_forward.1.refs_2_.refs_1_, ...), custom_call_target="tpu_custom_call" | custom-call | flops 2264924160 | bytes 23251968 | tf_op jit(solution)/shard_map/attention_backward/pallas_call | solution.py:42
  113.3 2.6 %projection_grads.1.refs_8_.refs_7_ = bf16[768,1536]{1,0:T(8,128)(2,1)S(1)} custom-call(bf16[768,768]{1,0:T(8,128)(2,1)S(1)} %get-tuple-element.131.refs_0_, bf16[768,1152]{1,0:T(8,128)(2,1)S(1)} %get-tuple-element.138.refs_1_, bf16[768,768]{1,0:T(8,128)(2,1)S(1)} %get-tuple-element.139.refs_2_, bf16[768,384]{1,0:T(8,128)(2,1)S(1)} %get-tuple-element.119.refs_0_.refs_3_), custom_call_target="tpu_custom_call" | custom-call | flops 1811939328 | bytes 7077888 | tf_op jit(solution)/shard_map/projection_grads/pallas_call | solution.py:42
  115.9 1.7 final_forward.1
  123.8 2.0 %final_backward.1 = (bf16[768,768]{1,0:T(8,128)(2,1)S(1)}, bf16[768,128]{1,0:T(8,128)(2,1)S(1)}) custom-call(bf16[768,768]{1,0:T(8,128)(2,1)S(1)} %bitcast.93, bf16[768,768]{1,0:T(8,128)(2,1)S(1)} %bitcast.103, f32[768,768]{1,0:T(8,128)S(1)} %get-tuple-element.161.refs_2_, bf16[768,768]{1,0:T(8,128)(2,1)S(1)} %get-tuple-element.162.refs_3_, ...), custom_call_target="tpu_custom_call" | custom-call | bytes 8530944 | tf_op jit(solution)/shard_map/final_backward/pallas_call | solution.py:42
  128.4 4.5 %collective-permute-done.31 = bf16[4,48,1024]{2,1,0:T(8,128)(2,1)S(1)} collective-permute-done((bf16[4,48,1024]{2,1,0:T(8,128)(2,1)S(1)}, bf16[4,48,1024]{2,1,0:T(8,128)(2,1)S(1)}, u32[]{:S(2)}, u32[]{:S(2)}) %collective-permute-start.31) | collective-permute-done | bytes 393248 | tf_op jit(solution)/shard_map/ppermute | solution.py:444
  136.3 4.8 %collective-permute-done.38 = bf16[8,48,512]{2,1,0:T(8,128)(2,1)S(1)} collective-permute-done((bf16[8,48,512]{2,1,0:T(8,128)(2,1)S(1)}, bf16[8,48,512]{2,1,0:T(8,128)(2,1)S(1)}, u32[]{:S(2)}, u32[]{:S(2)}) %collective-permute-start.38) | collective-permute-done | bytes 393248 | tf_op jit(solution)/shard_map/ppermute | solution.py:444
  142.3 2.7 %collective-permute-done.39 = bf16[8,48,512]{2,1,0:T(8,128)(2,1)S(1)} collective-permute-done((bf16[8,48,512]{2,1,0:T(8,128)(2,1)S(1)}, bf16[8,48,512]{2,1,0:T(8,128)(2,1)S(1)}, u32[]{:S(2)}, u32[]{:S(2)}) %collective-permute-start.39) | collective-permute-done | bytes 393248 | tf_op jit(solution)/shard_map/ppermute | solution.py:444
  150.9 5.0 %put_rows.2 = (bf16[3,2048,384]{2,1,0:T(8,128)(2,1)}, f32[8,128]{1,0:T(8,128)S(1)}) custom-call(s32[5]{0:T(128)S(1)} %pad_add_fusion.refs_0_, s32[3,256]{1,0:T(4,128)S(1)} %copy-done.5, bf16[768,768]{1,0:T(8,128)(2,1)S(1)} %get-tuple-element.140.refs_2_, bf16[3,2048,384]{2,1,0:T(8,128)(2,1)S(1)} %bitcast.105, ...), custom_call_target="tpu_custom_call" | custom-call | flops 1207959552 | bytes 9437184 | tf_op jit(solution)/shard_map/put_rows/pallas_call | solution.py:370
  159.1 2.8 %collective-permute-done.44 = bf16[2,48,512]{2,1,0:T(8,128)(2,1)S(1)} collective-permute-done((bf16[2,48,512]{2,1,0:T(8,128)(2,1)S(1)}, bf16[2,48,512]{2,1,0:T(8,128)(2,1)S(1)}, u32[]{:S(2)}, u32[]{:S(2)}) %collective-permute-start.44) | collective-permute-done | bytes 98336 | tf_op jit(solution)/shard_map/ppermute | solution.py:444
  162.4 2.5 %collective-permute-done.46 = bf16[2,48,640]{2,1,0:T(8,128)(2,1)S(1)} collective-permute-done((bf16[2,48,640]{2,1,0:T(8,128)(2,1)S(1)}, bf16[2,48,640]{2,1,0:T(8,128)(2,1)S(1)}, u32[]{:S(2)}, u32[]{:S(2)}) %collective-permute-start.46) | collective-permute-done | bytes 122912 | tf_op jit(solution)/shard_map/ppermute | solution.py:444
  167.1 5.0 %put_rows.3 = (bf16[3,2048,384]{2,1,0:T(8,128)(2,1)}, f32[8,128]{1,0:T(8,128)}) custom-call(s32[5]{0:T(128)S(1)} %pad_add_fusion.refs_0_, s32[3,256]{1,0:T(4,128)S(1)} %copy-done.5, bf16[768,768]{1,0:T(8,128)(2,1)S(1)} %get-tuple-element.165.refs_2_, bf16[3,2048,384]{2,1,0:T(8,128)(2,1)S(1)} %bitcast.107, f32[8,128]{1,0:T(8,128)S(1)} %get-tuple-element.166.refs_4_.refs_7_), custom_call_target="tpu_custom_call" | custom-call | flops 1207959552 | bytes 9437184 | tf_op jit(solution)/shard_map/put_rows/pallas_call | solution.py:370
  (150 shorter events, 57.3 us)
Async XLA Ops:
  3.1 12.7 %collective-permute-start = (bf16[1,48,1664]{2,1,0:T(8,128)(2,1)S(1)}, bf16[1,48,1664]{2,1,0:T(8,128)(2,1)S(1)}, u32[]{:S(2)}, u32[]{:S(2)}) collective-permute-start(bf16[1,48,1664]{2,1,0:T(8,128)(2,1)S(1)} %bitcast.149), channel_id=1, source_target_pairs={{0,16},{2,18},{4,20},{6,22},{8,24},{10,26},{12,28},{14,30},{16,0},... | collective-permute-start | bytes 479240 | tf_op jit(solution)/shard_map/ppermute | solution.py:444
  21.5 15.6 %collective-permute-start.5 = (bf16[1,48,3072]{2,1,0:T(8,128)(2,1)S(1)}, bf16[1,48,3072]{2,1,0:T(8,128)(2,1)S(1)}, u32[]{:S(2)}, u32[]{:S(2)}) collective-permute-start(bf16[1,48,3072]{2,1,0:T(8,128)(2,1)S(1)} %bitcast.122), channel_id=1, source_target_pairs={{0,16},{2,18},{4,20},{6,22},{8,24},{10,26},{12,28},{14,30},{16,0},... | collective-permute-start | bytes 884744 | tf_op jit(solution)/shard_map/ppermute | solution.py:444
  25.3 12.2 %collective-permute-start.7 = (bf16[4,48,640]{2,1,0:T(8,128)(2,1)S(1)}, bf16[4,48,640]{2,1,0:T(8,128)(2,1)S(1)}, u32[]{:S(2)}, u32[]{:S(2)}) collective-permute-start(bf16[4,48,640]{2,1,0:T(8,128)(2,1)S(1)} %bitcast.168), channel_id=1, source_target_pairs={{0,8},{2,10},{4,12},{6,14},{8,0},{10,2},{12,4},{14,6},{16,24},{18,... | collective-permute-start | bytes 737288 | tf_op jit(solution)/shard_map/ppermute | solution.py:444
  27.8 9.3 %collective-permute-start.6 = (bf16[4,48,512]{2,1,0:T(8,128)(2,1)S(1)}, bf16[4,48,512]{2,1,0:T(8,128)(2,1)S(1)}, u32[]{:S(2)}, u32[]{:S(2)}) collective-permute-start(bf16[4,48,512]{2,1,0:T(8,128)(2,1)S(1)} %bitcast.136), channel_id=1, source_target_pairs={{0,4},{2,6},{4,0},{6,2},{8,12},{10,14},{12,8},{14,10},{16,20},{18,... | collective-permute-start | bytes 589832 | tf_op jit(solution)/shard_map/ppermute | solution.py:444
  38.1 12.0 %collective-permute-start.12 = (bf16[8,48,512]{2,1,0:T(8,128)(2,1)S(1)}, bf16[8,48,512]{2,1,0:T(8,128)(2,1)S(1)}, u32[]{:S(2)}, u32[]{:S(2)}) collective-permute-start(bf16[8,48,512]{2,1,0:T(8,128)(2,1)S(1)} %bitcast.131), channel_id=1, source_target_pairs={{0,8},{2,10},{4,12},{6,14},{8,0},{10,2},{12,4},{14,6},{16,24},{18,... | collective-permute-start | bytes 1179656 | tf_op jit(solution)/shard_map/ppermute | solution.py:444
  38.3 13.6 %collective-permute-start.13 = (bf16[8,48,640]{2,1,0:T(8,128)(2,1)S(1)}, bf16[8,48,640]{2,1,0:T(8,128)(2,1)S(1)}, u32[]{:S(2)}, u32[]{:S(2)}) collective-permute-start(bf16[8,48,640]{2,1,0:T(8,128)(2,1)S(1)} %bitcast.153), channel_id=1, source_target_pairs={{0,2},{2,0},{4,6},{6,4},{8,10},{10,8},{12,14},{14,12},{16,18},{18,... | collective-permute-start | bytes 1474568 | tf_op jit(solution)/shard_map/ppermute | solution.py:444
  38.8 11.8 %collective-permute-start.14 = (bf16[8,48,512]{2,1,0:T(8,128)(2,1)S(1)}, bf16[8,48,512]{2,1,0:T(8,128)(2,1)S(1)}, u32[]{:S(2)}, u32[]{:S(2)}) collective-permute-start(bf16[8,48,512]{2,1,0:T(8,128)(2,1)S(1)} %bitcast.165), channel_id=1, source_target_pairs={{0,4},{2,6},{4,0},{6,2},{8,12},{10,14},{12,8},{14,10},{16,20},{18,... | collective-permute-start | bytes 1179656 | tf_op jit(solution)/shard_map/ppermute | solution.py:444
  40.2 12.4 %collective-permute-start.10 = (bf16[2,48,1024]{2,1,0:T(8,128)(2,1)S(1)}, bf16[2,48,1024]{2,1,0:T(8,128)(2,1)S(1)}, u32[]{:S(2)}, u32[]{:S(2)}) collective-permute-start(bf16[2,48,1024]{2,1,0:T(8,128)(2,1)S(1)} %get-tuple-element.111.refs_3_), channel_id=1, source_target_pairs={{0,4},{2,6},{4,0},{6,2},{8,12},{10,14},{12,8},{14,10},{16,20},{18,... | collective-permute-start | bytes 589832 | tf_op jit(solution)/shard_map/ppermute | solution.py:444
  41.6 11.0 %collective-permute-start.11 = (bf16[2,48,1024]{2,1,0:T(8,128)(2,1)S(1)}, bf16[2,48,1024]{2,1,0:T(8,128)(2,1)S(1)}, u32[]{:S(2)}, u32[]{:S(2)}) collective-permute-start(bf16[2,48,1024]{2,1,0:T(8,128)(2,1)S(1)} %get-tuple-element.112.refs_5_), channel_id=1, source_target_pairs={{0,8},{2,10},{4,12},{6,14},{8,0},{10,2},{12,4},{14,6},{16,24},{18,... | collective-permute-start | bytes 589832 | tf_op jit(solution)/shard_map/ppermute | solution.py:444
  63.4 17.6 %collective-permute-start.16 = (bf16[768,768]{1,0:T(8,128)(2,1)S(1)}, bf16[768,768]{1,0:T(8,128)(2,1)S(1)}, u32[]{:S(2)}, u32[]{:S(2)}) collective-permute-start(bf16[768,768]{1,0:T(8,128)(2,1)S(1)} %mix_forward.1.refs_2_.refs_1_), channel_id=1, source_target_pairs={{0,1},{1,0},{2,3},{3,2},{4,5},{5,4},{6,7},{7,6},{8,9},{9,8},{10,11... | collective-permute-start | bytes 3538952 | tf_op jit(solution)/shard_map/ppermute | solution.py:598
  65.9 12.1 %collective-permute-start.20 = (bf16[8,48,512]{2,1,0:T(8,128)(2,1)S(1)}, bf16[8,48,512]{2,1,0:T(8,128)(2,1)S(1)}, u32[]{:S(2)}, u32[]{:S(2)}) collective-permute-start(bf16[8,48,512]{2,1,0:T(8,128)(2,1)S(1)} %get-tuple-element.204.refs_1_), channel_id=1, source_target_pairs={{0,8},{2,10},{4,12},{6,14},{8,0},{10,2},{12,4},{14,6},{16,24},{18,... | collective-permute-start | bytes 1179656 | tf_op jit(solution)/shard_map/ppermute | solution.py:444
  67.7 10.8 %collective-permute-start.21 = (bf16[8,48,512]{2,1,0:T(8,128)(2,1)S(1)}, bf16[8,48,512]{2,1,0:T(8,128)(2,1)S(1)}, u32[]{:S(2)}, u32[]{:S(2)}) collective-permute-start(bf16[8,48,512]{2,1,0:T(8,128)(2,1)S(1)} %get-tuple-element.202.refs_3_), channel_id=1, source_target_pairs={{0,2},{2,0},{4,6},{6,4},{8,10},{10,8},{12,14},{14,12},{16,18},{18,... | collective-permute-start | bytes 1179656 | tf_op jit(solution)/shard_map/ppermute | solution.py:444
  68.4 11.9 %collective-permute-start.22 = (bf16[8,48,512]{2,1,0:T(8,128)(2,1)S(1)}, bf16[8,48,512]{2,1,0:T(8,128)(2,1)S(1)}, u32[]{:S(2)}, u32[]{:S(2)}) collective-permute-start(bf16[8,48,512]{2,1,0:T(8,128)(2,1)S(1)} %get-tuple-element.200.refs_5_), channel_id=1, source_target_pairs={{0,4},{2,6},{4,0},{6,2},{8,12},{10,14},{12,8},{14,10},{16,20},{18,... | collective-permute-start | bytes 1179656 | tf_op jit(solution)/shard_map/ppermute | solution.py:444
  70.0 17.7 %collective-permute-start.23 = (bf16[8,48,512]{2,1,0:T(8,128)(2,1)S(1)}, bf16[8,48,512]{2,1,0:T(8,128)(2,1)S(1)}, u32[]{:S(2)}, u32[]{:S(2)}) collective-permute-start(bf16[8,48,512]{2,1,0:T(8,128)(2,1)S(1)} %get-tuple-element.203.refs_1_), channel_id=1, source_target_pairs={{0,8},{2,10},{4,12},{6,14},{8,0},{10,2},{12,4},{14,6},{16,24},{18,... | collective-permute-start | bytes 1179656 | tf_op jit(solution)/shard_map/ppermute | solution.py:444
  78.0 9.7 %collective-permute-start.24 = (bf16[8,48,512]{2,1,0:T(8,128)(2,1)S(1)}, bf16[8,48,512]{2,1,0:T(8,128)(2,1)S(1)}, u32[]{:S(2)}, u32[]{:S(2)}) collective-permute-start(bf16[8,48,512]{2,1,0:T(8,128)(2,1)S(1)} %get-tuple-element.201.refs_3_), channel_id=1, source_target_pairs={{0,2},{2,0},{4,6},{6,4},{8,10},{10,8},{12,14},{14,12},{16,18},{18,... | collective-permute-start | bytes 1179656 | tf_op jit(solution)/shard_map/ppermute | solution.py:444
  78.5 9.2 %collective-permute-start.25 = (bf16[8,48,512]{2,1,0:T(8,128)(2,1)S(1)}, bf16[8,48,512]{2,1,0:T(8,128)(2,1)S(1)}, u32[]{:S(2)}, u32[]{:S(2)}) collective-permute-start(bf16[8,48,512]{2,1,0:T(8,128)(2,1)S(1)} %get-tuple-element.199.refs_5_), channel_id=1, source_target_pairs={{0,4},{2,6},{4,0},{6,2},{8,12},{10,14},{12,8},{14,10},{16,20},{18,... | collective-permute-start | bytes 1179656 | tf_op jit(solution)/shard_map/ppermute | solution.py:444
  92.4 9.1 %collective-permute-start.27 = (bf16[768,768]{1,0:T(8,128)(2,1)S(1)}, bf16[768,768]{1,0:T(8,128)(2,1)S(1)}, u32[]{:S(2)}, u32[]{:S(2)}) collective-permute-start(bf16[768,768]{1,0:T(8,128)(2,1)S(1)} %get-tuple-element.132.refs_3_), channel_id=1, source_target_pairs={{0,1},{1,0},{2,3},{3,2},{4,5},{5,4},{6,7},{7,6},{8,9},{9,8},{10,11... | collective-permute-start | bytes 3538952 | tf_op jit(solution)/shard_map/ppermute | solution.py:598
  96.3 19.6 %collective-permute-start.26 = (bf16[768,768]{1,0:T(8,128)(2,1)S(1)}, bf16[768,768]{1,0:T(8,128)(2,1)S(1)}, u32[]{:S(2)}, u32[]{:S(2)}) collective-permute-start(bf16[768,768]{1,0:T(8,128)(2,1)S(1)} %get-tuple-element.130.refs_1_.refs_4_), channel_id=1, source_target_pairs={{0,1},{1,0},{2,3},{3,2},{4,5},{5,4},{6,7},{7,6},{8,9},{9,8},{10,11... | collective-permute-start | bytes 3538952 | tf_op jit(solution)/shard_map/ppermute | solution.py:598
  97.9 19.7 %collective-permute-start.28 = (bf16[8,48,1024]{2,1,0:T(8,128)(2,1)S(1)}, bf16[8,48,1024]{2,1,0:T(8,128)(2,1)S(1)}, u32[]{:S(2)}, u32[]{:S(2)}) collective-permute-start(bf16[8,48,1024]{2,1,0:T(8,128)(2,1)S(1)} %get-tuple-element.141), channel_id=1, source_target_pairs={{0,8},{2,10},{4,12},{6,14},{8,0},{10,2},{12,4},{14,6},{16,24},{18,... | collective-permute-start | bytes 2359304 | tf_op jit(solution)/shard_map/ppermute | solution.py:444
  99.4 19.2 %collective-permute-start.29 = (bf16[8,48,1024]{2,1,0:T(8,128)(2,1)S(1)}, bf16[8,48,1024]{2,1,0:T(8,128)(2,1)S(1)}, u32[]{:S(2)}, u32[]{:S(2)}) collective-permute-start(bf16[8,48,1024]{2,1,0:T(8,128)(2,1)S(1)} %get-tuple-element.143), channel_id=1, source_target_pairs={{0,2},{2,0},{4,6},{6,4},{8,10},{10,8},{12,14},{14,12},{16,18},{18,... | collective-permute-start | bytes 2359304 | tf_op jit(solution)/shard_map/ppermute | solution.py:444
  101.0 18.9 %collective-permute-start.30 = (bf16[8,48,1024]{2,1,0:T(8,128)(2,1)S(1)}, bf16[8,48,1024]{2,1,0:T(8,128)(2,1)S(1)}, u32[]{:S(2)}, u32[]{:S(2)}) collective-permute-start(bf16[8,48,1024]{2,1,0:T(8,128)(2,1)S(1)} %get-tuple-element.145), channel_id=1, source_target_pairs={{0,4},{2,6},{4,0},{6,2},{8,12},{10,14},{12,8},{14,10},{16,20},{18,... | collective-permute-start | bytes 2359304 | tf_op jit(solution)/shard_map/ppermute | solution.py:444
  120.9 12.0 %collective-permute-start.31 = (bf16[4,48,1024]{2,1,0:T(8,128)(2,1)S(1)}, bf16[4,48,1024]{2,1,0:T(8,128)(2,1)S(1)}, u32[]{:S(2)}, u32[]{:S(2)}) collective-permute-start(bf16[4,48,1024]{2,1,0:T(8,128)(2,1)S(1)} %get-tuple-element.148), channel_id=1, source_target_pairs={{0,4},{2,6},{4,0},{6,2},{8,12},{10,14},{12,8},{14,10},{16,20},{18,... | collective-permute-start | bytes 1179656 | tf_op jit(solution)/shard_map/ppermute | solution.py:444
  121.5 12.0 %collective-permute-start.32 = (bf16[4,48,1024]{2,1,0:T(8,128)(2,1)S(1)}, bf16[4,48,1024]{2,1,0:T(8,128)(2,1)S(1)}, u32[]{:S(2)}, u32[]{:S(2)}) collective-permute-start(bf16[4,48,1024]{2,1,0:T(8,128)(2,1)S(1)} %get-tuple-element.150), channel_id=1, source_target_pairs={{0,8},{2,10},{4,12},{6,14},{8,0},{10,2},{12,4},{14,6},{16,24},{18,... | collective-permute-start | bytes 1179656 | tf_op jit(solution)/shard_map/ppermute | solution.py:444
  122.6 10.9 %collective-permute-start.33 = (bf16[4,48,1024]{2,1,0:T(8,128)(2,1)S(1)}, bf16[4,48,1024]{2,1,0:T(8,128)(2,1)S(1)}, u32[]{:S(2)}, u32[]{:S(2)}) collective-permute-start(bf16[4,48,1024]{2,1,0:T(8,128)(2,1)S(1)} %get-tuple-element.152), channel_id=1, source_target_pairs={{0,2},{2,0},{4,6},{6,4},{8,10},{10,8},{12,14},{14,12},{16,18},{18,... | collective-permute-start | bytes 1179656 | tf_op jit(solution)/shard_map/ppermute | solution.py:444
  126.5 18.4 %collective-permute-start.40 = (bf16[8,48,640]{2,1,0:T(8,128)(2,1)S(1)}, bf16[8,48,640]{2,1,0:T(8,128)(2,1)S(1)}, u32[]{:S(2)}, u32[]{:S(2)}) collective-permute-start(bf16[8,48,640]{2,1,0:T(8,128)(2,1)S(1)} %get-tuple-element.174), channel_id=1, source_target_pairs={{0,4},{2,6},{4,0},{6,2},{8,12},{10,14},{12,8},{14,10},{16,20},{18,... | collective-permute-start | bytes 1474568 | tf_op jit(solution)/shard_map/ppermute | solution.py:444
  127.1 14.0 %collective-permute-start.38 = (bf16[8,48,512]{2,1,0:T(8,128)(2,1)S(1)}, bf16[8,48,512]{2,1,0:T(8,128)(2,1)S(1)}, u32[]{:S(2)}, u32[]{:S(2)}) collective-permute-start(bf16[8,48,512]{2,1,0:T(8,128)(2,1)S(1)} %get-tuple-element.170), channel_id=1, source_target_pairs={{0,8},{2,10},{4,12},{6,14},{8,0},{10,2},{12,4},{14,6},{16,24},{18,... | collective-permute-start | bytes 1179656 | tf_op jit(solution)/shard_map/ppermute | solution.py:444
  132.9 12.1 %collective-permute-start.39 = (bf16[8,48,512]{2,1,0:T(8,128)(2,1)S(1)}, bf16[8,48,512]{2,1,0:T(8,128)(2,1)S(1)}, u32[]{:S(2)}, u32[]{:S(2)}) collective-permute-start(bf16[8,48,512]{2,1,0:T(8,128)(2,1)S(1)} %get-tuple-element.172), channel_id=1, source_target_pairs={{0,2},{2,0},{4,6},{6,4},{8,10},{10,8},{12,14},{14,12},{16,18},{18,... | collective-permute-start | bytes 1179656 | tf_op jit(solution)/shard_map/ppermute | solution.py:444
  134.3 14.2 %collective-permute-start.34 = (bf16[2,48,1024]{2,1,0:T(8,128)(2,1)S(1)}, bf16[2,48,1024]{2,1,0:T(8,128)(2,1)S(1)}, u32[]{:S(2)}, u32[]{:S(2)}) collective-permute-start(bf16[2,48,1024]{2,1,0:T(8,128)(2,1)S(1)} %get-tuple-element.154), channel_id=1, source_target_pairs={{0,2},{2,0},{4,6},{6,4},{8,10},{10,8},{12,14},{14,12},{16,18},{18,... | collective-permute-start | bytes 589832 | tf_op jit(solution)/shard_map/ppermute | solution.py:444
  135.8 13.3 %collective-permute-start.35 = (bf16[2,48,1024]{2,1,0:T(8,128)(2,1)S(1)}, bf16[2,48,1024]{2,1,0:T(8,128)(2,1)S(1)}, u32[]{:S(2)}, u32[]{:S(2)}) collective-permute-start(bf16[2,48,1024]{2,1,0:T(8,128)(2,1)S(1)} %get-tuple-element.156), channel_id=1, source_target_pairs={{0,4},{2,6},{4,0},{6,2},{8,12},{10,14},{12,8},{14,10},{16,20},{18,... | collective-permute-start | bytes 589832 | tf_op jit(solution)/shard_map/ppermute | solution.py:444
  145.8 10.4 %collective-permute-start.43 = (bf16[4,48,640]{2,1,0:T(8,128)(2,1)S(1)}, bf16[4,48,640]{2,1,0:T(8,128)(2,1)S(1)}, u32[]{:S(2)}, u32[]{:S(2)}) collective-permute-start(bf16[4,48,640]{2,1,0:T(8,128)(2,1)S(1)} %get-tuple-element.180), channel_id=1, source_target_pairs={{0,2},{2,0},{4,6},{6,4},{8,10},{10,8},{12,14},{14,12},{16,18},{18,... | collective-permute-start | bytes 737288 | tf_op jit(solution)/shard_map/ppermute | solution.py:444
  146.3 9.7 %collective-permute-start.41 = (bf16[4,48,512]{2,1,0:T(8,128)(2,1)S(1)}, bf16[4,48,512]{2,1,0:T(8,128)(2,1)S(1)}, u32[]{:S(2)}, u32[]{:S(2)}) collective-permute-start(bf16[4,48,512]{2,1,0:T(8,128)(2,1)S(1)} %get-tuple-element.176), channel_id=1, source_target_pairs={{0,4},{2,6},{4,0},{6,2},{8,12},{10,14},{12,8},{14,10},{16,20},{18,... | collective-permute-start | bytes 589832 | tf_op jit(solution)/shard_map/ppermute | solution.py:444
  149.7 16.5 %collective-permute-start.48 = (bf16[1,48,3072]{2,1,0:T(8,128)(2,1)S(1)}, bf16[1,48,3072]{2,1,0:T(8,128)(2,1)S(1)}, u32[]{:S(2)}, u32[]{:S(2)}) collective-permute-start(bf16[1,48,3072]{2,1,0:T(8,128)(2,1)S(1)} %get-tuple-element.191), channel_id=1, source_target_pairs={{0,16},{2,18},{4,20},{6,22},{8,24},{10,26},{12,28},{14,30},{16,0},... | collective-permute-start | bytes 884744 | tf_op jit(solution)/shard_map/ppermute | solution.py:444
  (30 other events, 189.2 us)

commit v2 on v1

--- a/solution.py
+++ b/solution.py
@@ -565,10 +565,11 @@
     return done
 
 
-def cut(cube, total):
+def cut(cube, total, ends=None):
     blocks = total.reshape(cube.count, -1, total.shape[1])
     bits = list(range(cube.depth))[::-1]
-    return [Part(blocks, bits, None, start, end - start) for start, end in thirds(total.shape[1]) if end > start]
+    ranges = ends or thirds(total.shape[1])
+    return [Part(blocks, bits, None, start, end - start) for start, end in ranges if end > start]
 
 
 def arrived(parts):
@@ -791,7 +792,8 @@
         scratch=[pltpu.VMEM((128, width), F32)],
         name="final_backward",
     )
-    first_grads = alone(cut(cube, first_grad))
+    ends = [half_width * k // 3 // 128 * 128 for k in (0, 5, 8, 12)]
+    first_grads = alone(cut(cube, first_grad, list(zip(ends, ends[1:]))))
     first_grads[-1] += cut(cube, vector_grads)
     first_grads = fold(cube, first_grads, back_bits(0))
     for step in range(2, steps):

time: 175 us -> 174 us (level)
  no operation moved by 1% of the time
where the time goes in v2:
time: 174 us
  Pallas kernels  68.9 us (40%)
  waiting for transfers between devices  48.9 us (28%)
  starting transfers between devices  45 us (26%)
  local copies, waits for them, and re-layouts  7.47 us (4%)
  other arithmetic  2.26 us (1%)
    pallas_call x32, Pallas kernels, call(): pl.pallas_call(body, out_shape=outs, in_specs=[pl.BlockSpec(memory_space=...  52.1 us
    ppermute x43, waiting for transfers between devices, swap(): lax.ppermute(value, 'dp', [(i, i ^ 1 << bit) for i in range(self.count)])  48.3 us
    ppermute x43, starting transfers between devices, swap(): lax.ppermute(value, 'dp', [(i, i ^ 1 << bit) for i in range(self.count)])  43.6 us
    pallas_call x2, Pallas kernels, put(): pl.pallas_call(body, grid=(rows, length // long), out_shape=(shape(base.s...  10 us
    pallas_call x2, Pallas kernels, select(): pl.pallas_call(body, grid=(rows,), out_shape=outs if mask else outs[:1],...  6.8 us
    unnamed x27, local copies, waits for them, and re-layouts  6.55 us
  transfers between devices with their start and end apart: 49, of which 24 were waited for; matrix products, arithmetic and copies ran while one was open for 1% of the time, Pallas kernels for 35%

profile of v2, /device:TPU:0, one launch (start us, length us, event | category | flops | bytes accessed | tf_op | source)
XLA Modules:
  0.0 173.6 jit_solution(14260657917034092491)
XLA Ops:
  3.1 4.1 %collective-permute-start = (bf16[1,48,1664]{2,1,0:T(8,128)(2,1)S(1)}, bf16[1,48,1664]{2,1,0:T(8,128)(2,1)S(1)}, u32[]{:S(2)}, u32[]{:S(2)}) collective-permute-start(bf16[1,48,1664]{2,1,0:T(8,128)(2,1)S(1)} %bitcast.148), channel_id=1, source_target_pairs={{0,16},{2,18},{4,20},{6,22},{8,24},{10,26},{12,28},{14,30},{16,0},... | collective-permute-start | bytes 479240 | tf_op jit(solution)/shard_map/ppermute | solution.py:444
  7.3 2.3 %copy-done = bf16[3,2048,384]{2,1,0:T(8,128)(2,1)S(1)} copy-done((bf16[3,2048,384]{2,1,0:T(8,128)(2,1)S(1)}, bf16[3,2048,384]{2,1,0:T(8,128)(2,1)}, u32[]{:S(2)}) %copy-start) | copy-done | bytes 4718616
  11.9 3.9 %select_rows.2 = (bf16[3,256,384]{2,1,0:T(8,128)(2,1)S(1)}, f32[3,256,256]{2,1,0:T(8,128)S(1)}, f32[768,1]{1,0:T(8,128)S(1)}) custom-call(bf16[3,2048,384]{2,1,0:T(8,128)(2,1)S(1)} %copy-done, s32[3,256]{1,0:T(4,128)S(1)} %copy-done.4, s32[3,2048]{1,0:T(4,128)S(1)} %copy-done.7, s32[3,2048]{1,0:T(4,128)S(1)} %copy-done.8), custom_call_target="tpu_custom_call" | custom-call | flops 1207959552 | bytes 4718592 | tf_op jit(solution)/shard_map/select_rows/pallas_call | solution.py:329
  16.8 1.6 collective-permute-start.2
  19.9 1.6 collective-permute-start.4
  25.3 2.5 %collective-permute-start.7 = (bf16[4,48,640]{2,1,0:T(8,128)(2,1)S(1)}, bf16[4,48,640]{2,1,0:T(8,128)(2,1)S(1)}, u32[]{:S(2)}, u32[]{:S(2)}) collective-permute-start(bf16[4,48,640]{2,1,0:T(8,128)(2,1)S(1)} %bitcast.169), channel_id=1, source_target_pairs={{0,8},{2,10},{4,12},{6,14},{8,0},{10,2},{12,4},{14,6},{16,24},{18,... | collective-permute-start | bytes 737288 | tf_op jit(solution)/shard_map/ppermute | solution.py:444
  28.9 2.9 %select_rows.3.refs_8_.refs_0_ = bf16[3,256,384]{2,1,0:T(8,128)(2,1)S(1)} custom-call(bf16[3,2048,384]{2,1,0:T(8,128)(2,1)S(1)} %bitcast.107, s32[3,256]{1,0:T(4,128)S(1)} %copy-done.5, bf16[4,48,512]{2,1,0:T(8,128)(2,1)S(1)} %bitcast.138), custom_call_target="tpu_custom_call" | custom-call | flops 1207959552 | bytes 4718592 | tf_op jit(solution)/shard_map/select_rows/pallas_call | solution.py:329
  31.7 5.3 %collective-permute-done.5.refs_2_.refs_7_ = bf16[1,48,3072]{2,1,0:T(8,128)(2,1)S(1)} collective-permute-done((bf16[1,48,3072]{2,1,0:T(8,128)(2,1)S(1)}, bf16[1,48,3072]{2,1,0:T(8,128)(2,1)S(1)}, u32[]{:S(2)}, u32[]{:S(2)}) %collective-permute-start.5) | collective-permute-done | bytes 294944 | tf_op jit(solution)/shard_map/ppermute | solution.py:444
  41.6 1.9 %collective-permute-start.11 = (bf16[2,48,1024]{2,1,0:T(8,128)(2,1)S(1)}, bf16[2,48,1024]{2,1,0:T(8,128)(2,1)S(1)}, u32[]{:S(2)}, u32[]{:S(2)}) collective-permute-start(bf16[2,48,1024]{2,1,0:T(8,128)(2,1)S(1)} %get-tuple-element.112.refs_5_), channel_id=1, source_target_pairs={{0,8},{2,10},{4,12},{6,14},{8,0},{10,2},{12,4},{14,6},{16,24},{18,... | collective-permute-start | bytes 589832 | tf_op jit(solution)/shard_map/ppermute | solution.py:444
  43.5 6.6 %collective-permute-done.12.refs_2_ = bf16[8,48,512]{2,1,0:T(8,128)(2,1)S(1)} collective-permute-done((bf16[8,48,512]{2,1,0:T(8,128)(2,1)S(1)}, bf16[8,48,512]{2,1,0:T(8,128)(2,1)S(1)}, u32[]{:S(2)}, u32[]{:S(2)}) %collective-permute-start.12) | collective-permute-done | bytes 393248 | tf_op jit(solution)/shard_map/ppermute | solution.py:444
  52.6 3.2 %collective-permute-done.9.refs_2_ = bf16[2,48,1024]{2,1,0:T(8,128)(2,1)S(1)} collective-permute-done((bf16[2,48,1024]{2,1,0:T(8,128)(2,1)S(1)}, bf16[2,48,1024]{2,1,0:T(8,128)(2,1)S(1)}, u32[]{:S(2)}, u32[]{:S(2)}) %collective-permute-start.9) | collective-permute-done | bytes 196640 | tf_op jit(solution)/shard_map/ppermute | solution.py:444
  57.9 4.7 %attention_forward.1 = (bf16[768,768]{1,0:T(8,128)(2,1)S(1)}, bf16[768,1152]{1,0:T(8,128)(2,1)S(1)}, f32[3,6,256,256]{3,2,1,0:T(8,128)S(1)}, bf16[768,384]{1,0:T(8,128)(2,1)S(1)}, f32[8,768]{1,0:T(8,128)S(1)}) custom-call(bf16[768,768]{1,0:T(8,128)(2,1)S(1)} %bitcast.89, bf16[768,1664]{1,0:T(8,128)(2,1)S(1)} %bitcast.86, ...), custom_call_target="tpu_custom_call" | custom-call | flops 1358954496 | bytes 12804096 | tf_op jit(solution)/shard_map/attention_forward/pallas_call | solution.py:42
  65.9 1.7 collective-permute-start.20
  68.4 1.6 collective-permute-start.22
  70.6 7.4 %collective-permute-done.20.refs_2_ = bf16[8,48,512]{2,1,0:T(8,128)(2,1)S(1)} collective-permute-done((bf16[8,48,512]{2,1,0:T(8,128)(2,1)S(1)}, bf16[8,48,512]{2,1,0:T(8,128)(2,1)S(1)}, u32[]{:S(2)}, u32[]{:S(2)}) %collective-permute-start.20) | collective-permute-done | bytes 393248 | tf_op jit(solution)/shard_map/ppermute | solution.py:444
  78.5 1.7 collective-permute-start.25
  81.0 6.6 %up_forward.1 = (bf16[768,768]{1,0:T(8,128)(2,1)S(1)}, bf16[768,1536]{1,0:T(8,128)(2,1)S(1)}, bf16[768,1536]{1,0:T(8,128)(2,1)S(1)}, bf16[768,768]{1,0:T(8,128)(2,1)S(1)}, bf16[768,1536]{1,0:T(8,128)(2,1)S(1)}) custom-call(bf16[768,768]{1,0:T(8,128)(2,1)S(1)} %bitcast.90, bf16[768,768]{1,0:T(8,128)(2,1)S(1)} %bitcast.100, ...), custom_call_target="tpu_custom_call" | custom-call | flops 3623878656 | bytes 16542720 | tf_op jit(solution)/shard_map/up_forward/pallas_call | solution.py:42
  88.4 3.9 %down_backward.1 = (bf16[768,1536]{1,0:T(8,128)(2,1)S(1)}, bf16[768,768]{1,0:T(8,128)(2,1)S(1)}) custom-call(bf16[768,768]{1,0:T(8,128)(2,1)S(1)} %get-tuple-element.126.refs_0_, bf16[768,1536]{1,0:T(8,128)(2,1)S(1)} %bitcast.124, bf16[768,1536]{1,0:T(8,128)(2,1)S(1)} %get-tuple-element.128.refs_2_, bf16[768,1536]{1,0:T(8,128)(2,1)S(1)} %bitcast.127), custom_call_target="tpu_custom_call" | custom-call | flops 3623878656 | bytes 11796480 | tf_op jit(solution)/shard_map/down_backward/pallas_call | solution.py:42
  92.5 3.8 %down_forward.1 = (bf16[768,1536]{1,0:T(8,128)(2,1)S(1)}, bf16[768,768]{1,0:T(8,128)(2,1)S(1)}) custom-call(bf16[768,768]{1,0:T(8,128)(2,1)S(1)} %get-tuple-element.125.refs_0_, bf16[768,1536]{1,0:T(8,128)(2,1)S(1)} %get-tuple-element.129.refs_1_, bf16[768,1536]{1,0:T(8,128)(2,1)S(1)} %get-tuple-element.127.refs_7_.refs_2_, bf16[768,1536]{1,0:T(8,128)(2,1)S(1)} %bitcast.125), custom_call_target="tpu_custom_call" | custom-call | flops 3623878656 | bytes 11796480 | tf_op jit(solution)/shard_map/down_forward/pallas_call | solution.py:42
  99.4 1.6 collective-permute-start.29
  101.5 11.7 %attention_backward.1 = (bf16[768,768]{1,0:T(8,128)(2,1)S(1)}, bf16[768,1152]{1,0:T(8,128)(2,1)S(1)}, bf16[768,768]{1,0:T(8,128)(2,1)S(1)}, f32[768,768]{1,0:T(8,128)S(1)}, f32[8,768]{1,0:T(8,128)S(1)}) custom-call(bf16[768,768]{1,0:T(8,128)(2,1)S(1)} %bitcast.91, bf16[768,768]{1,0:T(8,128)(2,1)S(1)} %mix_forward.1.refs_2_.refs_1_, ...), custom_call_target="tpu_custom_call" | custom-call | flops 2264924160 | bytes 23251968 | tf_op jit(solution)/shard_map/attention_backward/pallas_call | solution.py:42
  113.3 2.6 %projection_grads.1.refs_8_.refs_7_ = bf16[768,1536]{1,0:T(8,128)(2,1)S(1)} custom-call(bf16[768,768]{1,0:T(8,128)(2,1)S(1)} %get-tuple-element.131.refs_0_, bf16[768,1152]{1,0:T(8,128)(2,1)S(1)} %get-tuple-element.138.refs_1_, bf16[768,768]{1,0:T(8,128)(2,1)S(1)} %get-tuple-element.139.refs_2_, bf16[768,384]{1,0:T(8,128)(2,1)S(1)} %get-tuple-element.119.refs_0_.refs_3_), custom_call_target="tpu_custom_call" | custom-call | flops 1811939328 | bytes 7077888 | tf_op jit(solution)/shard_map/projection_grads/pallas_call | solution.py:42
  115.9 1.7 final_forward.1
  123.8 2.2 %final_backward.1 = (bf16[768,768]{1,0:T(8,128)(2,1)S(1)}, bf16[768,128]{1,0:T(8,128)(2,1)S(1)}) custom-call(bf16[768,768]{1,0:T(8,128)(2,1)S(1)} %bitcast.93, bf16[768,768]{1,0:T(8,128)(2,1)S(1)} %bitcast.103, f32[768,768]{1,0:T(8,128)S(1)} %get-tuple-element.161.refs_2_, bf16[768,768]{1,0:T(8,128)(2,1)S(1)} %get-tuple-element.162.refs_3_, ...), custom_call_target="tpu_custom_call" | custom-call | bytes 8530944 | tf_op jit(solution)/shard_map/final_backward/pallas_call | solution.py:42
  128.7 4.3 %collective-permute-done.31 = bf16[4,48,1024]{2,1,0:T(8,128)(2,1)S(1)} collective-permute-done((bf16[4,48,1024]{2,1,0:T(8,128)(2,1)S(1)}, bf16[4,48,1024]{2,1,0:T(8,128)(2,1)S(1)}, u32[]{:S(2)}, u32[]{:S(2)}) %collective-permute-start.31) | collective-permute-done | bytes 393248 | tf_op jit(solution)/shard_map/ppermute | solution.py:444
  136.4 6.5 %collective-permute-done.39 = bf16[8,48,384]{2,1,0:T(8,128)(2,1)S(1)} collective-permute-done((bf16[8,48,384]{2,1,0:T(8,128)(2,1)S(1)}, bf16[8,48,384]{2,1,0:T(8,128)(2,1)S(1)}, u32[]{:S(2)}, u32[]{:S(2)}) %collective-permute-start.39) | collective-permute-done | bytes 294944 | tf_op jit(solution)/shard_map/ppermute | solution.py:444
  144.9 1.6 collective-permute-start.41
  147.7 1.9 %collective-permute-done.36 = bf16[2,48,1024]{2,1,0:T(8,128)(2,1)S(1)} collective-permute-done((bf16[2,48,1024]{2,1,0:T(8,128)(2,1)S(1)}, bf16[2,48,1024]{2,1,0:T(8,128)(2,1)S(1)}, u32[]{:S(2)}, u32[]{:S(2)}) %collective-permute-start.36) | collective-permute-done | bytes 196640 | tf_op jit(solution)/shard_map/ppermute | solution.py:444
  150.6 5.0 %put_rows.2 = (bf16[3,2048,384]{2,1,0:T(8,128)(2,1)}, f32[8,128]{1,0:T(8,128)S(1)}) custom-call(s32[5]{0:T(128)S(1)} %pad_add_fusion.refs_0_, s32[3,256]{1,0:T(4,128)S(1)} %copy-done.5, bf16[768,768]{1,0:T(8,128)(2,1)S(1)} %get-tuple-element.140.refs_2_, bf16[3,2048,384]{2,1,0:T(8,128)(2,1)S(1)} %bitcast.105, ...), custom_call_target="tpu_custom_call" | custom-call | flops 1207959552 | bytes 9437184 | tf_op jit(solution)/shard_map/put_rows/pallas_call | solution.py:370
  159.3 3.0 %collective-permute-done.45 = bf16[2,48,384]{2,1,0:T(8,128)(2,1)S(1)} collective-permute-done((bf16[2,48,384]{2,1,0:T(8,128)(2,1)S(1)}, bf16[2,48,384]{2,1,0:T(8,128)(2,1)S(1)}, u32[]{:S(2)}, u32[]{:S(2)}) %collective-permute-start.45) | collective-permute-done | bytes 73760 | tf_op jit(solution)/shard_map/ppermute | solution.py:444
  162.2 2.6 %collective-permute-done.46 = bf16[2,48,640]{2,1,0:T(8,128)(2,1)S(1)} collective-permute-done((bf16[2,48,640]{2,1,0:T(8,128)(2,1)S(1)}, bf16[2,48,640]{2,1,0:T(8,128)(2,1)S(1)}, u32[]{:S(2)}, u32[]{:S(2)}) %collective-permute-start.46) | collective-permute-done | bytes 122912 | tf_op jit(solution)/shard_map/ppermute | solution.py:444
  167.2 5.0 %put_rows.3 = (bf16[3,2048,384]{2,1,0:T(8,128)(2,1)}, f32[8,128]{1,0:T(8,128)}) custom-call(s32[5]{0:T(128)S(1)} %pad_add_fusion.refs_0_, s32[3,256]{1,0:T(4,128)S(1)} %copy-done.5, bf16[768,768]{1,0:T(8,128)(2,1)S(1)} %get-tuple-element.165.refs_2_, bf16[3,2048,384]{2,1,0:T(8,128)(2,1)S(1)} %bitcast.107, f32[8,128]{1,0:T(8,128)S(1)} %get-tuple-element.166.refs_4_.refs_7_), custom_call_target="tpu_custom_call" | custom-call | flops 1207959552 | bytes 9437184 | tf_op jit(solution)/shard_map/put_rows/pallas_call | solution.py:370
  (150 shorter events, 55.4 us)
Async XLA Ops:
  3.1 12.7 %collective-permute-start = (bf16[1,48,1664]{2,1,0:T(8,128)(2,1)S(1)}, bf16[1,48,1664]{2,1,0:T(8,128)(2,1)S(1)}, u32[]{:S(2)}, u32[]{:S(2)}) collective-permute-start(bf16[1,48,1664]{2,1,0:T(8,128)(2,1)S(1)} %bitcast.148), channel_id=1, source_target_pairs={{0,16},{2,18},{4,20},{6,22},{8,24},{10,26},{12,28},{14,30},{16,0},... | collective-permute-start | bytes 479240 | tf_op jit(solution)/shard_map/ppermute | solution.py:444
  21.5 15.6 %collective-permute-start.5 = (bf16[1,48,3072]{2,1,0:T(8,128)(2,1)S(1)}, bf16[1,48,3072]{2,1,0:T(8,128)(2,1)S(1)}, u32[]{:S(2)}, u32[]{:S(2)}) collective-permute-start(bf16[1,48,3072]{2,1,0:T(8,128)(2,1)S(1)} %bitcast.122), channel_id=1, source_target_pairs={{0,16},{2,18},{4,20},{6,22},{8,24},{10,26},{12,28},{14,30},{16,0},... | collective-permute-start | bytes 884744 | tf_op jit(solution)/shard_map/ppermute | solution.py:444
  25.3 12.2 %collective-permute-start.7 = (bf16[4,48,640]{2,1,0:T(8,128)(2,1)S(1)}, bf16[4,48,640]{2,1,0:T(8,128)(2,1)S(1)}, u32[]{:S(2)}, u32[]{:S(2)}) collective-permute-start(bf16[4,48,640]{2,1,0:T(8,128)(2,1)S(1)} %bitcast.169), channel_id=1, source_target_pairs={{0,8},{2,10},{4,12},{6,14},{8,0},{10,2},{12,4},{14,6},{16,24},{18,... | collective-permute-start | bytes 737288 | tf_op jit(solution)/shard_map/ppermute | solution.py:444
  27.8 9.3 %collective-permute-start.6 = (bf16[4,48,512]{2,1,0:T(8,128)(2,1)S(1)}, bf16[4,48,512]{2,1,0:T(8,128)(2,1)S(1)}, u32[]{:S(2)}, u32[]{:S(2)}) collective-permute-start(bf16[4,48,512]{2,1,0:T(8,128)(2,1)S(1)} %bitcast.137), channel_id=1, source_target_pairs={{0,4},{2,6},{4,0},{6,2},{8,12},{10,14},{12,8},{14,10},{16,20},{18,... | collective-permute-start | bytes 589832 | tf_op jit(solution)/shard_map/ppermute | solution.py:444
  38.1 12.0 %collective-permute-start.12 = (bf16[8,48,512]{2,1,0:T(8,128)(2,1)S(1)}, bf16[8,48,512]{2,1,0:T(8,128)(2,1)S(1)}, u32[]{:S(2)}, u32[]{:S(2)}) collective-permute-start(bf16[8,48,512]{2,1,0:T(8,128)(2,1)S(1)} %bitcast.131), channel_id=1, source_target_pairs={{0,8},{2,10},{4,12},{6,14},{8,0},{10,2},{12,4},{14,6},{16,24},{18,... | collective-permute-start | bytes 1179656 | tf_op jit(solution)/shard_map/ppermute | solution.py:444
  38.3 13.6 %collective-permute-start.13 = (bf16[8,48,640]{2,1,0:T(8,128)(2,1)S(1)}, bf16[8,48,640]{2,1,0:T(8,128)(2,1)S(1)}, u32[]{:S(2)}, u32[]{:S(2)}) collective-permute-start(bf16[8,48,640]{2,1,0:T(8,128)(2,1)S(1)} %bitcast.155), channel_id=1, source_target_pairs={{0,2},{2,0},{4,6},{6,4},{8,10},{10,8},{12,14},{14,12},{16,18},{18,... | collective-permute-start | bytes 1474568 | tf_op jit(solution)/shard_map/ppermute | solution.py:444
  38.8 11.8 %collective-permute-start.14 = (bf16[8,48,512]{2,1,0:T(8,128)(2,1)S(1)}, bf16[8,48,512]{2,1,0:T(8,128)(2,1)S(1)}, u32[]{:S(2)}, u32[]{:S(2)}) collective-permute-start(bf16[8,48,512]{2,1,0:T(8,128)(2,1)S(1)} %bitcast.163), channel_id=1, source_target_pairs={{0,4},{2,6},{4,0},{6,2},{8,12},{10,14},{12,8},{14,10},{16,20},{18,... | collective-permute-start | bytes 1179656 | tf_op jit(solution)/shard_map/ppermute | solution.py:444
  40.2 12.4 %collective-permute-start.10 = (bf16[2,48,1024]{2,1,0:T(8,128)(2,1)S(1)}, bf16[2,48,1024]{2,1,0:T(8,128)(2,1)S(1)}, u32[]{:S(2)}, u32[]{:S(2)}) collective-permute-start(bf16[2,48,1024]{2,1,0:T(8,128)(2,1)S(1)} %get-tuple-element.111.refs_3_), channel_id=1, source_target_pairs={{0,4},{2,6},{4,0},{6,2},{8,12},{10,14},{12,8},{14,10},{16,20},{18,... | collective-permute-start | bytes 589832 | tf_op jit(solution)/shard_map/ppermute | solution.py:444
  41.6 11.0 %collective-permute-start.11 = (bf16[2,48,1024]{2,1,0:T(8,128)(2,1)S(1)}, bf16[2,48,1024]{2,1,0:T(8,128)(2,1)S(1)}, u32[]{:S(2)}, u32[]{:S(2)}) collective-permute-start(bf16[2,48,1024]{2,1,0:T(8,128)(2,1)S(1)} %get-tuple-element.112.refs_5_), channel_id=1, source_target_pairs={{0,8},{2,10},{4,12},{6,14},{8,0},{10,2},{12,4},{14,6},{16,24},{18,... | collective-permute-start | bytes 589832 | tf_op jit(solution)/shard_map/ppermute | solution.py:444
  63.4 17.6 %collective-permute-start.16 = (bf16[768,768]{1,0:T(8,128)(2,1)S(1)}, bf16[768,768]{1,0:T(8,128)(2,1)S(1)}, u32[]{:S(2)}, u32[]{:S(2)}) collective-permute-start(bf16[768,768]{1,0:T(8,128)(2,1)S(1)} %mix_forward.1.refs_2_.refs_1_), channel_id=1, source_target_pairs={{0,1},{1,0},{2,3},{3,2},{4,5},{5,4},{6,7},{7,6},{8,9},{9,8},{10,11... | collective-permute-start | bytes 3538952 | tf_op jit(solution)/shard_map/ppermute | solution.py:599
  65.9 12.1 %collective-permute-start.20 = (bf16[8,48,512]{2,1,0:T(8,128)(2,1)S(1)}, bf16[8,48,512]{2,1,0:T(8,128)(2,1)S(1)}, u32[]{:S(2)}, u32[]{:S(2)}) collective-permute-start(bf16[8,48,512]{2,1,0:T(8,128)(2,1)S(1)} %get-tuple-element.204.refs_1_), channel_id=1, source_target_pairs={{0,8},{2,10},{4,12},{6,14},{8,0},{10,2},{12,4},{14,6},{16,24},{18,... | collective-permute-start | bytes 1179656 | tf_op jit(solution)/shard_map/ppermute | solution.py:444
  67.7 10.8 %collective-permute-start.21 = (bf16[8,48,512]{2,1,0:T(8,128)(2,1)S(1)}, bf16[8,48,512]{2,1,0:T(8,128)(2,1)S(1)}, u32[]{:S(2)}, u32[]{:S(2)}) collective-permute-start(bf16[8,48,512]{2,1,0:T(8,128)(2,1)S(1)} %get-tuple-element.202.refs_3_), channel_id=1, source_target_pairs={{0,2},{2,0},{4,6},{6,4},{8,10},{10,8},{12,14},{14,12},{16,18},{18,... | collective-permute-start | bytes 1179656 | tf_op jit(solution)/shard_map/ppermute | solution.py:444
  68.4 11.9 %collective-permute-start.22 = (bf16[8,48,512]{2,1,0:T(8,128)(2,1)S(1)}, bf16[8,48,512]{2,1,0:T(8,128)(2,1)S(1)}, u32[]{:S(2)}, u32[]{:S(2)}) collective-permute-start(bf16[8,48,512]{2,1,0:T(8,128)(2,1)S(1)} %get-tuple-element.200.refs_5_), channel_id=1, source_target_pairs={{0,4},{2,6},{4,0},{6,2},{8,12},{10,14},{12,8},{14,10},{16,20},{18,... | collective-permute-start | bytes 1179656 | tf_op jit(solution)/shard_map/ppermute | solution.py:444
  70.0 17.7 %collective-permute-start.23 = (bf16[8,48,512]{2,1,0:T(8,128)(2,1)S(1)}, bf16[8,48,512]{2,1,0:T(8,128)(2,1)S(1)}, u32[]{:S(2)}, u32[]{:S(2)}) collective-permute-start(bf16[8,48,512]{2,1,0:T(8,128)(2,1)S(1)} %get-tuple-element.203.refs_1_), channel_id=1, source_target_pairs={{0,8},{2,10},{4,12},{6,14},{8,0},{10,2},{12,4},{14,6},{16,24},{18,... | collective-permute-start | bytes 1179656 | tf_op jit(solution)/shard_map/ppermute | solution.py:444
  78.0 9.7 %collective-permute-start.24 = (bf16[8,48,512]{2,1,0:T(8,128)(2,1)S(1)}, bf16[8,48,512]{2,1,0:T(8,128)(2,1)S(1)}, u32[]{:S(2)}, u32[]{:S(2)}) collective-permute-start(bf16[8,48,512]{2,1,0:T(8,128)(2,1)S(1)} %get-tuple-element.201.refs_3_), channel_id=1, source_target_pairs={{0,2},{2,0},{4,6},{6,4},{8,10},{10,8},{12,14},{14,12},{16,18},{18,... | collective-permute-start | bytes 1179656 | tf_op jit(solution)/shard_map/ppermute | solution.py:444
  78.5 9.2 %collective-permute-start.25 = (bf16[8,48,512]{2,1,0:T(8,128)(2,1)S(1)}, bf16[8,48,512]{2,1,0:T(8,128)(2,1)S(1)}, u32[]{:S(2)}, u32[]{:S(2)}) collective-permute-start(bf16[8,48,512]{2,1,0:T(8,128)(2,1)S(1)} %get-tuple-element.199.refs_5_), channel_id=1, source_target_pairs={{0,4},{2,6},{4,0},{6,2},{8,12},{10,14},{12,8},{14,10},{16,20},{18,... | collective-permute-start | bytes 1179656 | tf_op jit(solution)/shard_map/ppermute | solution.py:444
  92.4 9.1 %collective-permute-start.27 = (bf16[768,768]{1,0:T(8,128)(2,1)S(1)}, bf16[768,768]{1,0:T(8,128)(2,1)S(1)}, u32[]{:S(2)}, u32[]{:S(2)}) collective-permute-start(bf16[768,768]{1,0:T(8,128)(2,1)S(1)} %get-tuple-element.132.refs_3_), channel_id=1, source_target_pairs={{0,1},{1,0},{2,3},{3,2},{4,5},{5,4},{6,7},{7,6},{8,9},{9,8},{10,11... | collective-permute-start | bytes 3538952 | tf_op jit(solution)/shard_map/ppermute | solution.py:599
  96.3 19.6 %collective-permute-start.26 = (bf16[768,768]{1,0:T(8,128)(2,1)S(1)}, bf16[768,768]{1,0:T(8,128)(2,1)S(1)}, u32[]{:S(2)}, u32[]{:S(2)}) collective-permute-start(bf16[768,768]{1,0:T(8,128)(2,1)S(1)} %get-tuple-element.130.refs_1_.refs_4_), channel_id=1, source_target_pairs={{0,1},{1,0},{2,3},{3,2},{4,5},{5,4},{6,7},{7,6},{8,9},{9,8},{10,11... | collective-permute-start | bytes 3538952 | tf_op jit(solution)/shard_map/ppermute | solution.py:599
  97.9 19.7 %collective-permute-start.28 = (bf16[8,48,1024]{2,1,0:T(8,128)(2,1)S(1)}, bf16[8,48,1024]{2,1,0:T(8,128)(2,1)S(1)}, u32[]{:S(2)}, u32[]{:S(2)}) collective-permute-start(bf16[8,48,1024]{2,1,0:T(8,128)(2,1)S(1)} %get-tuple-element.141), channel_id=1, source_target_pairs={{0,8},{2,10},{4,12},{6,14},{8,0},{10,2},{12,4},{14,6},{16,24},{18,... | collective-permute-start | bytes 2359304 | tf_op jit(solution)/shard_map/ppermute | solution.py:444
  99.4 19.2 %collective-permute-start.29 = (bf16[8,48,1024]{2,1,0:T(8,128)(2,1)S(1)}, bf16[8,48,1024]{2,1,0:T(8,128)(2,1)S(1)}, u32[]{:S(2)}, u32[]{:S(2)}) collective-permute-start(bf16[8,48,1024]{2,1,0:T(8,128)(2,1)S(1)} %get-tuple-element.143), channel_id=1, source_target_pairs={{0,2},{2,0},{4,6},{6,4},{8,10},{10,8},{12,14},{14,12},{16,18},{18,... | collective-permute-start | bytes 2359304 | tf_op jit(solution)/shard_map/ppermute | solution.py:444
  101.0 18.9 %collective-permute-start.30 = (bf16[8,48,1024]{2,1,0:T(8,128)(2,1)S(1)}, bf16[8,48,1024]{2,1,0:T(8,128)(2,1)S(1)}, u32[]{:S(2)}, u32[]{:S(2)}) collective-permute-start(bf16[8,48,1024]{2,1,0:T(8,128)(2,1)S(1)} %get-tuple-element.145), channel_id=1, source_target_pairs={{0,4},{2,6},{4,0},{6,2},{8,12},{10,14},{12,8},{14,10},{16,20},{18,... | collective-permute-start | bytes 2359304 | tf_op jit(solution)/shard_map/ppermute | solution.py:444
  121.0 12.0 %collective-permute-start.31 = (bf16[4,48,1024]{2,1,0:T(8,128)(2,1)S(1)}, bf16[4,48,1024]{2,1,0:T(8,128)(2,1)S(1)}, u32[]{:S(2)}, u32[]{:S(2)}) collective-permute-start(bf16[4,48,1024]{2,1,0:T(8,128)(2,1)S(1)} %get-tuple-element.148), channel_id=1, source_target_pairs={{0,4},{2,6},{4,0},{6,2},{8,12},{10,14},{12,8},{14,10},{16,20},{18,... | collective-permute-start | bytes 1179656 | tf_op jit(solution)/shard_map/ppermute | solution.py:444
  121.6 12.0 %collective-permute-start.32 = (bf16[4,48,1024]{2,1,0:T(8,128)(2,1)S(1)}, bf16[4,48,1024]{2,1,0:T(8,128)(2,1)S(1)}, u32[]{:S(2)}, u32[]{:S(2)}) collective-permute-start(bf16[4,48,1024]{2,1,0:T(8,128)(2,1)S(1)} %get-tuple-element.150), channel_id=1, source_target_pairs={{0,8},{2,10},{4,12},{6,14},{8,0},{10,2},{12,4},{14,6},{16,24},{18,... | collective-permute-start | bytes 1179656 | tf_op jit(solution)/shard_map/ppermute | solution.py:444
  122.7 10.9 %collective-permute-start.33 = (bf16[4,48,1024]{2,1,0:T(8,128)(2,1)S(1)}, bf16[4,48,1024]{2,1,0:T(8,128)(2,1)S(1)}, u32[]{:S(2)}, u32[]{:S(2)}) collective-permute-start(bf16[4,48,1024]{2,1,0:T(8,128)(2,1)S(1)} %get-tuple-element.152), channel_id=1, source_target_pairs={{0,2},{2,0},{4,6},{6,4},{8,10},{10,8},{12,14},{14,12},{16,18},{18,... | collective-permute-start | bytes 1179656 | tf_op jit(solution)/shard_map/ppermute | solution.py:444
  126.9 17.2 %collective-permute-start.38 = (bf16[8,48,640]{2,1,0:T(8,128)(2,1)S(1)}, bf16[8,48,640]{2,1,0:T(8,128)(2,1)S(1)}, u32[]{:S(2)}, u32[]{:S(2)}) collective-permute-start(bf16[8,48,640]{2,1,0:T(8,128)(2,1)S(1)} %get-tuple-element.170), channel_id=1, source_target_pairs={{0,8},{2,10},{4,12},{6,14},{8,0},{10,2},{12,4},{14,6},{16,24},{18,... | collective-permute-start | bytes 1474568 | tf_op jit(solution)/shard_map/ppermute | solution.py:444
  128.0 16.0 %collective-permute-start.40 = (bf16[8,48,640]{2,1,0:T(8,128)(2,1)S(1)}, bf16[8,48,640]{2,1,0:T(8,128)(2,1)S(1)}, u32[]{:S(2)}, u32[]{:S(2)}) collective-permute-start(bf16[8,48,640]{2,1,0:T(8,128)(2,1)S(1)} %get-tuple-element.174), channel_id=1, source_target_pairs={{0,4},{2,6},{4,0},{6,2},{8,12},{10,14},{12,8},{14,10},{16,20},{18,... | collective-permute-start | bytes 1474568 | tf_op jit(solution)/shard_map/ppermute | solution.py:444
  133.0 9.9 %collective-permute-start.39 = (bf16[8,48,384]{2,1,0:T(8,128)(2,1)S(1)}, bf16[8,48,384]{2,1,0:T(8,128)(2,1)S(1)}, u32[]{:S(2)}, u32[]{:S(2)}) collective-permute-start(bf16[8,48,384]{2,1,0:T(8,128)(2,1)S(1)} %get-tuple-element.172), channel_id=1, source_target_pairs={{0,2},{2,0},{4,6},{6,4},{8,10},{10,8},{12,14},{14,12},{16,18},{18,... | collective-permute-start | bytes 884744 | tf_op jit(solution)/shard_map/ppermute | solution.py:444
  134.4 12.5 %collective-permute-start.34 = (bf16[2,48,1024]{2,1,0:T(8,128)(2,1)S(1)}, bf16[2,48,1024]{2,1,0:T(8,128)(2,1)S(1)}, u32[]{:S(2)}, u32[]{:S(2)}) collective-permute-start(bf16[2,48,1024]{2,1,0:T(8,128)(2,1)S(1)} %get-tuple-element.154), channel_id=1, source_target_pairs={{0,2},{2,0},{4,6},{6,4},{8,10},{10,8},{12,14},{14,12},{16,18},{18,... | collective-permute-start | bytes 589832 | tf_op jit(solution)/shard_map/ppermute | solution.py:444
  135.9 11.8 %collective-permute-start.35 = (bf16[2,48,1024]{2,1,0:T(8,128)(2,1)S(1)}, bf16[2,48,1024]{2,1,0:T(8,128)(2,1)S(1)}, u32[]{:S(2)}, u32[]{:S(2)}) collective-permute-start(bf16[2,48,1024]{2,1,0:T(8,128)(2,1)S(1)} %get-tuple-element.156), channel_id=1, source_target_pairs={{0,4},{2,6},{4,0},{6,2},{8,12},{10,14},{12,8},{14,10},{16,20},{18,... | collective-permute-start | bytes 589832 | tf_op jit(solution)/shard_map/ppermute | solution.py:444
  144.9 10.7 %collective-permute-start.41 = (bf16[4,48,640]{2,1,0:T(8,128)(2,1)S(1)}, bf16[4,48,640]{2,1,0:T(8,128)(2,1)S(1)}, u32[]{:S(2)}, u32[]{:S(2)}) collective-permute-start(bf16[4,48,640]{2,1,0:T(8,128)(2,1)S(1)} %get-tuple-element.176), channel_id=1, source_target_pairs={{0,4},{2,6},{4,0},{6,2},{8,12},{10,14},{12,8},{14,10},{16,20},{18,... | collective-permute-start | bytes 737288 | tf_op jit(solution)/shard_map/ppermute | solution.py:444
  146.4 9.1 %collective-permute-start.43 = (bf16[4,48,640]{2,1,0:T(8,128)(2,1)S(1)}, bf16[4,48,640]{2,1,0:T(8,128)(2,1)S(1)}, u32[]{:S(2)}, u32[]{:S(2)}) collective-permute-start(bf16[4,48,640]{2,1,0:T(8,128)(2,1)S(1)} %get-tuple-element.180), channel_id=1, source_target_pairs={{0,2},{2,0},{4,6},{6,4},{8,10},{10,8},{12,14},{14,12},{16,18},{18,... | collective-permute-start | bytes 737288 | tf_op jit(solution)/shard_map/ppermute | solution.py:444
  150.3 16.1 %collective-permute-start.48 = (bf16[1,48,3072]{2,1,0:T(8,128)(2,1)S(1)}, bf16[1,48,3072]{2,1,0:T(8,128)(2,1)S(1)}, u32[]{:S(2)}, u32[]{:S(2)}) collective-permute-start(bf16[1,48,3072]{2,1,0:T(8,128)(2,1)S(1)} %get-tuple-element.191), channel_id=1, source_target_pairs={{0,16},{2,18},{4,20},{6,22},{8,24},{10,26},{12,28},{14,30},{16,0},... | collective-permute-start | bytes 884744 | tf_op jit(solution)/shard_map/ppermute | solution.py:444
  (30 other events, 188.7 us)
